TPU v7x, 32 devices: a whole 2x2x4 slice. The times are simulated.
32 devices in a mesh: grp: 4 (over y, x), dev: 8 (over z, core).
Axes of the slice: x: 2, y: 2, z: 4, core: 2. Of those that a mesh axis runs over, the one named last changes fastest.
Arguments:
- embedding: bfloat16 [32768, 256], P(('grp', 'dev')), may hold values from -6 to 6
- cotangent: bfloat16 [32768, 256], P(('grp', 'dev')), may hold values from -6 to 6
- fractional: bfloat16 [3, 32768], P(None, ('grp', 'dev')), may hold values from 0 to 1
- wave_index: int32 [3, 512], replicated, may hold values from -8 to 8
- tile_pairs: int32 [768, 2], P(('grp', 'dev')), may hold values from 0 to 15, as said below
- counts: int32 [32], P(('grp', 'dev')), may hold values from 3 to 24, as said below
- wave_filter: float32 [512, 256], replicated, may hold values from -0.25 to 0.25
- short_weight: bfloat16 [256, 256], replicated, may hold values from -0.375 to 0.375
Outputs:
- message: bfloat16 [32768, 256], P(('grp', 'dev'))
- embedding_grad: bfloat16 [32768, 256], P(('grp', 'dev'))
Inputs may be any that keep to these rules, and one draw needn't show every extreme that they name: `tile_pairs`: in each block's 24 rows, column 0 is one of the block's 8 tiles and column 1 one of 16 tiles: the block's own, then the next block's. The first row of every block names a tile of the next block. `counts`: some block has exactly 24 live rows in every draw.
All inputs are finite; a program needn't handle non-finite values.
Results may differ from a plain program's by a relative error of at most 0.0059.
Values may be sent and summed in bfloat16 or wider, within the bound.
A program may use at most 64 MiB of HBM per device.

v0:
```python
import math

import jax
import jax.numpy as jnp
from jax import lax
from jax.sharding import PartitionSpec as P

TILE = 128


two_pi = 2.0 * math.pi


def shifted(value, axis, by):
    size = lax.axis_size(axis)
    return lax.ppermute(value, axis, [(i, (i + by) % size) for i in range(size)])


def trig_table(places, wave_index):
    phase = two_pi * jnp.dot(
        places.astype(jnp.float32).T,
        wave_index.astype(jnp.float32),
        precision=lax.Precision.HIGHEST,
    )
    return jnp.concatenate([jnp.cos(phase), jnp.sin(phase)], axis=1).astype(jnp.bfloat16)


def pair_kernel(left_places, right_places):
    left = left_places.astype(jnp.float32)
    right = right_places.astype(jnp.float32)
    wave = jnp.sin(math.pi * (left[:, :, None] - right[:, None, :]))
    spread = jnp.exp(-2.0 * jnp.sum(wave * wave, axis=0))
    return (spread / math.sqrt(left.shape[1])).astype(jnp.bfloat16)


def pair_kernels(place_tiles, firsts, seconds):
    return jax.vmap(pair_kernel)(place_tiles[firsts], place_tiles[seconds])


def one_hot_rows(indices, keep, width):
    hits = (indices[:, None] == jnp.arange(width, dtype=jnp.int32)[None, :]) & keep[:, None]
    return hits.astype(jnp.float32)


def collect(hot, terms):
    return jnp.einsum("pt,pic->tic", hot, terms, precision=lax.Precision.HIGHEST)


def body(
    embedding, cotangent, fractional, wave_index, tile_pairs, counts, wave_filter, short_weight
):
    atom_rows, channels = embedding.shape
    wave_count = wave_index.shape[1]
    tile_count = atom_rows // TILE
    pair_rows = tile_pairs.shape[0]
    blocks = lax.axis_size("grp") * lax.axis_size("dev")
    inv_root = 1.0 / math.sqrt(atom_rows * blocks)
    table = trig_table(fractional, wave_index)
    joined = jnp.concatenate([embedding, cotangent], axis=1)
    rows = 2 * wave_count // lax.axis_size("dev")
    columns = table
    within = lax.psum_scatter(
        lax.dot_general(
            columns, joined, (((0,), (0,)), ((), ())), preferred_element_type=jnp.float32
        ),
        "dev",
        scatter_dimension=0,
        tiled=True,
    )
    summed = lax.psum(within, "grp")
    local = lax.dynamic_slice_in_dim(
        wave_filter, lax.axis_index("dev") * rows % wave_count, summed.shape[0], 0
    )
    tiled = jnp.concatenate([local, local], axis=1)
    coeffs = (summed * tiled * inv_root).astype(jnp.bfloat16)
    columns = table
    long_range = jnp.dot(
        columns,
        lax.all_gather(coeffs, "dev", axis=0, tiled=True),
        preferred_element_type=jnp.float32,
    )
    projected = jnp.dot(embedding, short_weight, preferred_element_type=jnp.float32).astype(
        jnp.bfloat16
    )
    above_projected, above_places = shifted((projected, fractional), ("grp", "dev"), -1)
    near_projected = jnp.concatenate([projected, above_projected], axis=0).reshape(
        2 * tile_count, TILE, channels
    )
    near_places = (
        jnp.concatenate([fractional, above_places], axis=1)
        .reshape(3, 2 * tile_count, TILE)
        .transpose(1, 0, 2)
    )
    cotangent_tiles = cotangent.reshape(tile_count, TILE, channels)
    firsts = tile_pairs[:, 0]
    seconds = tile_pairs[:, 1]
    live = jnp.arange(pair_rows, dtype=jnp.int32) < counts[0]
    kernels = pair_kernels(near_places, firsts, seconds)
    ahead = jnp.einsum(
        "pij,pjc->pic", kernels, near_projected[seconds], preferred_element_type=jnp.float32
    )
    behind = jnp.einsum(
        "pij,pic->pjc", kernels, cotangent_tiles[firsts], preferred_element_type=jnp.float32
    )
    forward = collect(one_hot_rows(firsts, live, tile_count), ahead)
    backward = collect(one_hot_rows(seconds, live, 2 * tile_count), behind)
    below = shifted(backward[tile_count:].astype(jnp.bfloat16), ("grp", "dev"), 1).astype(
        jnp.float32
    )
    own_back = backward[:tile_count]
    near_grad = (own_back + below).reshape(atom_rows, channels).astype(jnp.bfloat16)
    message = (long_range[:, :channels] + forward.reshape(atom_rows, channels)).astype(jnp.bfloat16)
    mixed = lax.dot_general(
        near_grad, short_weight, (((1,), (1,)), ((), ())), preferred_element_type=jnp.float32
    )
    embedding_grad = (long_range[:, channels:] + mixed).astype(jnp.bfloat16)
    return (message, embedding_grad)


def solution(mesh):
    in_specs = (
        P(("grp", "dev"), None),
        P(("grp", "dev"), None),
        P(None, ("grp", "dev")),
        P(),
        P(("grp", "dev"), None),
        P(("grp", "dev")),
        P(),
        P(),
    )
    out_specs = (P(("grp", "dev"), None), P(("grp", "dev"), None))
    return jax.shard_map(body, mesh=mesh, in_specs=in_specs, out_specs=out_specs, check_vma=False)
```

profile of v0, /device:TPU:0, one launch (start us, length us, event | category | flops | bytes accessed | tf_op | source)
XLA Modules:
  0.0 149.8 jit_solution(6674804931434613379)
XLA Ops:
  7.2 0.0 copy-start
  7.2 0.0 copy-start.4
  7.2 0.0 reduce-scatter.2.cloned.1.call-start
  7.2 10.6 %cosine_convert_fusion = (bf16[1024,512]{0,1:T(8,128)(2,1)S(1)}, bf16[1024,512]{0,1:T(8,128)(2,1)}) fusion(bf16[3,1024]{1,0:T(4,128)(2,1)} %param.10, s32[3,512]{1,0:T(4,128)} %param.11), kind=kOutput, calls=%fused_computation.11 | convolution fusion | flops 20448768 | bytes 2109440 | tf_op jit(solution)/shard_map/dot_general | solution.py:20
  17.8 1.0 copy-done.7
  18.8 3.8 %fusion.5 = f32[1024,512]{1,0:T(8,128)} fusion(bf16[1024,512]{0,1:T(8,128)(2,1)} %get-tuple-element.3, bf16[1024,512]{0,1:T(8,128)(2,1)S(1)} %get-tuple-element.2, bf16[1024,256]{1,0:T(8,128)(2,1)S(1)} %copy-done.4, bf16[1024,256]{1,0:T(8,128)(2,1)S(1)} %copy-done.10), kind=kOutput, calls=%fused_computation.15 | convolution fusion | flops 1080033280 | bytes 5242880 | tf_op jit(solution)/shard_map/dot_general | solution.py:63
  22.6 0.0 reduce-scatter.2.cloned.1.call-update
  22.7 0.0 all-reduce.2.cloned.1.call-start
  22.7 0.6 copy-done.11
  23.3 6.4 %collective-permute-start = (bf16[3,1024]{1,0:T(4,128)(2,1)S(1)}, bf16[3,1024]{1,0:T(4,128)(2,1)S(1)}, u32[]{:S(2)}, u32[]{:S(2)}) collective-permute-start(bf16[3,1024]{1,0:T(4,128)(2,1)S(1)} %copy-done.11), channel_id=1, source_target_pairs={{0,31},{1,0},{2,1},{3,2},{4,3},{5,4},{6,5},{7,6},{8,7},{9,8},{10,9... | collective-permute-start | bytes 18440 | tf_op jit(solution)/shard_map/ppermute | solution.py:16
  29.7 0.0 copy-done.9
  29.7 0.3 convolution_convert_fusion
  30.0 0.0 copy-start.5
  30.0 0.7 collective-permute-start.1
  31.5 0.0 copy-done
  31.5 0.6 gather_fusion.3
  32.2 0.0 collective-permute-done
  32.2 0.6 gather_fusion
  32.8 0.6 gather_fusion.1
  33.4 29.8 %reduce-scatter.2.cloned.1.call-done = f32[128,512]{1,0:T(8,128)} async-done(((f32[1024,512]{1,0:T(8,128)}), f32[128,512]{1,0:T(8,128)}) %reduce-scatter.2.cloned.1.call-update) | async-done | bytes 262160 | tf_op jit(solution)/shard_map/reduce_scatter | solution.py:62
  63.3 0.0 all-reduce.2.cloned.1.call-update
  63.3 0.0 all-gather.2.cloned.1.call-start
  63.3 17.8 %multiply_reduce_fusion = f32[24,128,128]{2,1,0:T(8,128)} fusion(f32[24,3,128]{2,1,0:T(4,128)S(1)} %convert_element_type.49, f32[24,3,128]{2,1,0:T(4,128)S(1)} %convert_element_type.48), kind=kLoop, calls=%fused_computation.4 | loop fusion | flops 4325376 | bytes 1646592 | tf_op jit(solution)/shard_map/vmap()/reduce_sum | solution.py:32
  81.2 27.0 %all-reduce.2.cloned.1.call-done = f32[128,512]{1,0:T(8,128)} async-done(((f32[128,512]{1,0:T(8,128)}), f32[128,512]{1,0:T(8,128)}) %all-reduce.2.cloned.1.call-update) | async-done | bytes 262160 | tf_op jit(solution)/shard_map/psum | solution.py:70
  108.1 1.6 %fusion.13 = bf16[128,512]{1,0:T(8,128)(2,1)} fusion(f32[128,512]{1,0:T(8,128)} %all-reduce.2.cloned.1.call-done, f32[128,256]{1,0:T(8,128)S(1)} %constant_dynamic-slice_fusion), kind=kLoop, calls=%fused_computation.29 | loop fusion | flops 262144 | bytes 524288 | tf_op jit(solution)/shard_map/convert_element_type | solution.py:75
  109.8 0.0 all-gather.2.cloned.1.call-update
  109.8 2.0 %fusion.14 = f32[24,128,256]{2,1,0:T(8,128)S(1)} fusion(bf16[24,128,256]{2,1,0:T(8,128)(2,1)S(1)} %gather_fusion.3, f32[24,128,128]{2,1,0:T(8,128)} %multiply_reduce_fusion), kind=kOutput, calls=%fused_computation.30 | convolution fusion | flops 202506240 | bytes 6291456 | tf_op jit(solution)/shard_map/pij,pic->pjc/dot_general | solution.py:102
  111.8 0.0 copy-start.6
  111.9 3.1 %fusion = f32[16,128,256]{2,0,1:T(8,128)S(1)} fusion(f32[24,128,256]{2,1,0:T(8,128)S(1)} %fusion.14, s32[24]{0:T(128)S(1)} %get-tuple-element.4, pred[24]{0:T(512)(128)(4,1)S(1)} %iota_compare_fusion.2), kind=kOutput, calls=%fused_computation.5 | convolution fusion | flops 150995712 | bytes 5243000 | tf_op jit(solution)/shard_map/pt,pic->tic/dot_general | solution.py:46
  115.0 0.9 slice.50
  115.9 0.0 collective-permute-start.2
  115.9 0.6 copy-done.1
  116.5 0.0 collective-permute-done.1
  116.5 0.0 copy-done.6
  116.5 1.1 pad_maximum_fusion.3
  117.6 0.0 copy-start.3
  117.7 1.9 %gather_fusion.2 = bf16[24,128,256]{2,1,0:T(8,128)(2,1)} fusion(bf16[16,128,256]{2,1,0:T(8,128)(2,1)S(1)} %bitcast.35, s32[1024]{0:T(1024)S(1)} %pad_clamp_fusion.1), kind=kCustom, calls=%fused_computation.2 | custom fusion | bytes 3145824 | tf_op jit(solution)/shard_map/gather | solution.py:100
  119.5 2.0 %fusion.15 = f32[24,128,256]{2,1,0:T(8,128)S(1)} fusion(bf16[24,128,256]{2,1,0:T(8,128)(2,1)} %gather_fusion.2, f32[24,128,128]{2,1,0:T(8,128)S(1)} %copy-done.3), kind=kOutput, calls=%fused_computation.31 | convolution fusion | flops 202506240 | bytes 6291456 | tf_op jit(solution)/shard_map/pij,pjc->pic/dot_general | solution.py:99
  121.5 2.9 %fusion.2 = f32[8,128,256]{2,0,1:T(8,128)S(1)} fusion(f32[24,128,256]{2,1,0:T(8,128)S(1)} %fusion.15, s32[24]{0:T(128)S(1)} %get-tuple-element.8, pred[24]{0:T(512)(128)(4,1)S(1)} %iota_compare_fusion.2), kind=kOutput, calls=%fused_computation.7 | convolution fusion | flops 75497856 | bytes 4194424 | tf_op jit(solution)/shard_map/pt,pic->tic/dot_general | solution.py:46
  124.4 0.0 copy-start.2
  124.4 0.3 copy.16
  124.7 12.1 %collective-permute-done.2 = bf16[8,128,256]{2,0,1:T(8,128)(2,1)} collective-permute-done((bf16[8,128,256]{2,0,1:T(8,128)(2,1)}, bf16[8,128,256]{2,0,1:T(8,128)(2,1)}, u32[]{:S(2)}, u32[]{:S(2)}) %collective-permute-start.2) | collective-permute-done | bytes 524320 | tf_op jit(solution)/shard_map/ppermute | solution.py:16
  136.9 1.2 fusion.7
  138.1 0.1 copy.19
  138.2 0.0 all-gather.2.cloned.1.call-done
  138.3 2.8 %fusion.4 = f32[1024,512]{1,0:T(8,128)S(1)} fusion(bf16[1024,512]{1,0:T(8,128)(2,1)} %all-gather.2.cloned.1.call-done, bf16[1024,512]{0,1:T(8,128)(2,1)} %get-tuple-element.3, bf16[1024,512]{0,1:T(8,128)(2,1)S(1)} %copy-done.8), kind=kOutput, calls=%fused_computation.14 | convolution fusion | flops 1077936128 | bytes 5242880 | tf_op jit(solution)/shard_map/dot_general | solution.py:77
  141.1 1.0 fusion.8
  142.1 1.1 fusion.6
  (23 shorter events, 0.1 us)
Async XLA Ops:
  7.2 24.3 %copy-start = (f32[512,256]{1,0:T(8,128)S(1)}, f32[512,256]{1,0:T(8,128)}, u32[]{:S(2)}) copy-start(f32[512,256]{1,0:T(8,128)} %param.14) | copy-start | bytes 1572868
  7.2 11.6 %copy-start.4 = (bf16[1024,256]{1,0:T(8,128)(2,1)S(1)}, bf16[1024,256]{1,0:T(8,128)(2,1)}, u32[]{:S(2)}) copy-start(bf16[1024,256]{1,0:T(8,128)(2,1)} %param.9) | copy-start | bytes 1572868
  7.2 11.6 %copy-start.10 = (bf16[1024,256]{1,0:T(8,128)(2,1)S(1)}, bf16[1024,256]{1,0:T(8,128)(2,1)}, u32[]{:S(2)}) copy-start(bf16[1024,256]{1,0:T(8,128)(2,1)} %param.8) | copy-start | bytes 1572868
  7.2 56.1 %reduce-scatter.2.cloned.1.call-start = ((), (), s32[]{:S(2)}) async-start(), calls=%async_computation.1 | async-start | bytes 2359296 | tf_op jit(solution)/shard_map/reduce_scatter | solution.py:62
  17.8 1.0 copy-start.7
  22.6 0.7 copy-start.11
  22.6 7.1 %copy-start.9 = (bf16[256,256]{1,0:T(8,128)(2,1)S(1)}, bf16[256,256]{1,0:T(8,128)(2,1)}, u32[]{:S(2)}) copy-start(bf16[256,256]{1,0:T(8,128)(2,1)} %param.15) | copy-start | bytes 393220
  22.6 8.8 %copy-start.12 = (s32[24,2]{0,1:T(2,128)S(1)}, s32[24,2]{0,1:T(2,128)}, u32[]{:S(2)}) copy-start(s32[24,2]{0,1:T(2,128)} %param.12) | copy-start | bytes 580
  22.7 85.5 %all-reduce.2.cloned.1.call-start = ((), (), s32[]{:S(2)}) async-start(), calls=%async_computation.2 | async-start | bytes 524288 | tf_op jit(solution)/shard_map/psum | solution.py:70
  23.3 8.8 %collective-permute-start = (bf16[3,1024]{1,0:T(4,128)(2,1)S(1)}, bf16[3,1024]{1,0:T(4,128)(2,1)S(1)}, u32[]{:S(2)}, u32[]{:S(2)}) collective-permute-start(bf16[3,1024]{1,0:T(4,128)(2,1)S(1)} %copy-done.11), channel_id=1, source_target_pairs={{0,31},{1,0},{2,1},{3,2},{4,3},{5,4},{6,5},{7,6},{8,7},{9,8},{10,9... | collective-permute-start | bytes 18440 | tf_op jit(solution)/shard_map/ppermute | solution.py:16
  30.0 51.2 %copy-start.5 = (bf16[1024,256]{1,0:T(8,128)(2,1)}, bf16[1024,256]{1,0:T(8,128)(2,1)S(1)}, u32[]{:S(2)}) copy-start(bf16[1024,256]{1,0:T(8,128)(2,1)S(1)} %convolution_convert_fusion) | copy-start | bytes 1572868
  30.0 86.5 %collective-permute-start.1 = (bf16[1024,256]{1,0:T(8,128)(2,1)S(1)}, bf16[1024,256]{1,0:T(8,128)(2,1)}, u32[]{:S(2)}, u32[]{:S(2)}) collective-permute-start(bf16[1024,256]{1,0:T(8,128)(2,1)S(1)} %convolution_convert_fusion), channel_id=1, source_target_pairs={{0,31},{1,0},{2,1},{3,2},{4,3},{5,4},{6,5},{7,6},{8,7},{9,8},{10,9... | collective-permute-start | bytes 1572872 | tf_op jit(solution)/shard_map/ppermute | solution.py:16
  63.3 75.0 %all-gather.2.cloned.1.call-start = ((), (), s32[]{:S(2)}) async-start(), calls=%async_computation.3 | async-start | bytes 1179648 | tf_op jit(solution)/shard_map/all_gather | solution.py:79
  111.8 4.7 %copy-start.6 = (bf16[1024,256]{1,0:T(8,128)(2,1)S(1)}, bf16[1024,256]{1,0:T(8,128)(2,1)}, u32[]{:S(2)}) copy-start(bf16[1024,256]{1,0:T(8,128)(2,1)} %copy-done.5) | copy-start | bytes 1572868
  115.0 1.5 %copy-start.1 = (f32[16,128,256]{2,0,1:T(8,128)}, f32[16,128,256]{2,0,1:T(8,128)S(1)}, u32[]{:S(2)}) copy-start(f32[16,128,256]{2,0,1:T(8,128)S(1)} %fusion) | copy-start | bytes 6291460
  115.9 20.9 %collective-permute-start.2 = (bf16[8,128,256]{2,0,1:T(8,128)(2,1)}, bf16[8,128,256]{2,0,1:T(8,128)(2,1)}, u32[]{:S(2)}, u32[]{:S(2)}) collective-permute-start(bf16[8,128,256]{2,0,1:T(8,128)(2,1)} %slice.50), channel_id=1, source_target_pairs={{0,1},{1,2},{2,3},{3,4},{4,5},{5,6},{6,7},{7,8},{8,9},{9,10},{10,1... | collective-permute-start | bytes 1572872 | tf_op jit(solution)/shard_map/ppermute | solution.py:16
  117.6 1.9 %copy-start.3 = (f32[24,128,128]{2,1,0:T(8,128)S(1)}, f32[24,128,128]{2,1,0:T(8,128)}, u32[]{:S(2)}) copy-start(f32[24,128,128]{2,1,0:T(8,128)} %multiply_reduce_fusion) | copy-start | bytes 4718596
  124.4 12.5 %copy-start.2 = (f32[16,128,256]{2,0,1:T(8,128)S(1)}, f32[16,128,256]{2,0,1:T(8,128)}, u32[]{:S(2)}) copy-start(f32[16,128,256]{2,0,1:T(8,128)} %copy-done.1) | copy-start | bytes 6291460
  124.7 13.5 %copy-start.8 = (bf16[1024,512]{0,1:T(8,128)(2,1)S(1)}, bf16[1024,512]{0,1:T(8,128)(2,1)}, u32[]{:S(2)}) copy-start(bf16[1024,512]{0,1:T(8,128)(2,1)} %copy-done.7) | copy-start | bytes 3145732
Sparse Core Ops, SparseCore 0:
  22.8 40.4 reduce-scatter.1
  66.2 41.9 all-reduce.1
  109.9 24.7 all-gather.1
where the time goes:
time: 150 us
  waiting for transfers between devices  69 us (46%)
  matrix products  28.7 us (19%)
  other arithmetic  22.9 us (15%)
  between operations  14.7 us (10%)
  local copies, waits for them, and re-layouts  7.32 us (5%)
  starting transfers between devices  7.22 us (5%)
    reduce_scatter x1, waiting for transfers between devices, body(): lax.psum_scatter(lax.dot_general(columns, joined, (((0,), (0,)), ((), ())...  29.8 us
    psum x1, waiting for transfers between devices, body(): summed = lax.psum(within, 'grp')  27 us
    reduce_sum x1, other arithmetic, pair_kernel(): spread = jnp.exp(-2.0 * jnp.sum(wave * wave, axis=0))  17.8 us
    ppermute x3, waiting for transfers between devices, shifted(): lax.ppermute(value, axis, [(i, (i + by) % size) for i in range(size)])  12.1 us
    dot_general x1, matrix products, trig_table(): jnp.dot(places.astype(jnp.float32).T, wave_index.astype(jnp.float32), pre...  10.6 us
    ppermute x3, starting transfers between devices, shifted(): lax.ppermute(value, axis, [(i, (i + by) % size) for i in range(size)])  7.11 us
    dot_general x2, matrix products, collect(): jnp.einsum('pt,pic->tic', hot, terms, precision=lax.Precision.HIGHEST)  6.01 us
    dot_general x1, matrix products, body(): lax.dot_general(columns, joined, (((0,), (0,)), ((), ())), preferred_elem...  3.82 us
  transfers between devices with their start and end apart: 6, of which 3 were waited for; matrix products, arithmetic and copies ran while one was open for 25% of the time, Pallas kernels for 0%

commit v1 on v0

v1 whole, which is shorter than its diff:
```python
import math

import jax
import jax.numpy as jnp
from jax import lax
from jax.sharding import PartitionSpec as P

TILE = 128
two_pi = 2.0 * math.pi


def shifted(value, axis, by):
    size = lax.axis_size(axis)
    return lax.ppermute(value, axis, [(i, (i + by) % size) for i in range(size)])


def cos_sin(turns):
    rest = turns - jnp.round(turns)
    angle = rest * (two_pi / 4.0)
    sq = angle * angle
    sine = angle * (1.0 + sq * (-1.0 / 6 + sq * (1.0 / 120 + sq * (-1.0 / 5040 + sq * (1.0 / 362880)))))
    cosine = 1.0 + sq * (-0.5 + sq * (1.0 / 24 + sq * (-1.0 / 720 + sq * (1.0 / 40320))))
    for _ in range(2):
        sine, cosine = 2.0 * sine * cosine, 1.0 - 2.0 * sine * sine
    return cosine, sine


def trig_table(places, wave_index):
    turns = lax.dot_general(
        places, wave_index.astype(jnp.bfloat16), (((0,), (0,)), ((), ())), preferred_element_type=jnp.float32
    )
    cosine, sine = cos_sin(turns)
    return jnp.concatenate([cosine.astype(jnp.bfloat16), sine.astype(jnp.bfloat16)], axis=1)


def body(embedding, cotangent, fractional, wave_index, tile_pairs, counts, wave_filter, short_weight):
    atom_rows, channels = embedding.shape
    wave_count = wave_index.shape[1]
    tiles = atom_rows // TILE
    pair_rows = tile_pairs.shape[0]
    blocks = lax.axis_size("grp") * lax.axis_size("dev")
    inv_root = 1.0 / math.sqrt(atom_rows * blocks)
    above_embedding, above_places = shifted((embedding, fractional), ("grp", "dev"), -1)
    table = trig_table(fractional, wave_index)
    joined = jnp.concatenate([embedding, cotangent], axis=1)
    rows = 2 * wave_count // lax.axis_size("dev")
    within = lax.psum_scatter(
        lax.dot_general(table, joined, (((0,), (0,)), ((), ())), preferred_element_type=jnp.float32),
        "dev", scatter_dimension=0, tiled=True,
    )
    summed = lax.psum(within, "grp")
    local = lax.dynamic_slice_in_dim(wave_filter, lax.axis_index("dev") * rows % wave_count, rows, 0)
    coeffs = (summed * jnp.concatenate([local, local], axis=1) * inv_root).astype(jnp.bfloat16)
    coeffs = lax.all_gather(coeffs, "dev", axis=0, tiled=True)

    sources = jnp.dot(
        jnp.concatenate([embedding, above_embedding], axis=0), short_weight, preferred_element_type=jnp.float32
    ).astype(jnp.bfloat16)
    cosine, sine = cos_sin(jnp.concatenate([fractional, above_places], axis=1).astype(jnp.float32))
    waves = jnp.concatenate([cosine, sine], axis=0)
    closeness = lax.dot_general(
        waves[:, :atom_rows], waves, (((0,), (0,)), ((), ())), precision=lax.Precision.HIGHEST
    )
    live = (jnp.arange(pair_rows, dtype=jnp.int32) < counts[0])[:, None]
    first_hot = ((tile_pairs[:, :1] == jnp.arange(tiles, dtype=jnp.int32)) & live).astype(jnp.float32)
    second_hot = (tile_pairs[:, 1:] == jnp.arange(2 * tiles, dtype=jnp.int32)).astype(jnp.float32)
    times = jnp.einsum("pu,pv->uv", first_hot, second_hot)
    spread = (jnp.exp(closeness - 3.0) * (1.0 / math.sqrt(TILE))).astype(jnp.bfloat16)
    times = jnp.repeat(jnp.repeat(times, TILE, axis=0), TILE, axis=1).astype(jnp.bfloat16)
    weights = spread * times
    forward = jnp.dot(weights, sources, preferred_element_type=jnp.float32)
    backward = lax.dot_general(weights, cotangent, (((0,), (0,)), ((), ())), preferred_element_type=jnp.float32)
    below = shifted(backward[atom_rows:].astype(jnp.bfloat16), ("grp", "dev"), 1).astype(jnp.float32)
    near_grad = (backward[:atom_rows] + below).astype(jnp.bfloat16)
    mixed = lax.dot_general(near_grad, short_weight, (((1,), (1,)), ((), ())), preferred_element_type=jnp.float32)
    long_range = jnp.dot(table, coeffs, preferred_element_type=jnp.float32)
    message = (long_range[:, :channels] + forward).astype(jnp.bfloat16)
    embedding_grad = (long_range[:, channels:] + mixed).astype(jnp.bfloat16)
    return (message, embedding_grad)


def solution(mesh):
    split = P(("grp", "dev"), None)
    in_specs = (split, split, P(None, ("grp", "dev")), P(), split, P(("grp", "dev")), P(), P())
    return jax.shard_map(body, mesh=mesh, in_specs=in_specs, out_specs=(split, split), check_vma=False)
```

time: 150 us -> 144 us (0.960)
  other arithmetic: 22.9 us -> 1.77 us
  waiting for transfers between devices: 69 us -> 82.7 us
    reduce_sum x1 -> x0, other arithmetic: 17.8 us -> none  [pair_kernel(): spread = jnp.exp(-2.0 * jnp.sum(wave * wave, axis=0))]
    psum x1, waiting for transfers between devices: 27 us -> 44.7 us  [body(): summed = lax.psum(within, 'grp')]
    ppermute x3, waiting for transfers between devices: 12.1 us -> 0.01 us  [shifted(): lax.ppermute(value, axis, [(i, (i + by) % size) for i in range(size)])]
    all_gather x1, waiting for transfers between devices: 0.02 us -> 5.78 us  [body(): coeffs = lax.all_gather(coeffs, 'dev', axis=0, tiled=True)]
    broadcast_in_dim x0 -> x2, local copies, waits for them, and re-layouts: none -> 4.5 us  [the longest x1 4.46 us: body(): jnp.repeat(jnp.repeat(times, TILE, axis=0), TILE, axis=1)]
    gather x4 -> x0, local copies, waits for them, and re-layouts: 3.7 us -> none  [the longest x1 1.86 us: body(): near_projected[seconds]]
    reduce_scatter x1, waiting for transfers between devices: 29.8 us -> 32.2 us  [body(): lax.psum_scatter(lax.dot_general(table, joined, (((0,), (0,)), ((), ())),...]
    convert_element_type x5 -> x1, other arithmetic: 3.89 us -> 1.64 us  [body(): (summed * jnp.concatenate([local, local], axis=1) * inv_root).astype(jnp....]
  transfers between devices with their start and end apart: 6 -> 6, of which waited for: 3 -> 3; matrix products, arithmetic and copies ran while one was open for 25% -> 19% of each run, Pallas kernels for 0% -> 0%
where the time goes in v1:
time: 144 us
  waiting for transfers between devices  82.7 us (57%)
  matrix products  29.9 us (21%)
  between operations  14.5 us (10%)
  local copies, waits for them, and re-layouts  7.96 us (6%)
  starting transfers between devices  7.16 us (5%)
  other arithmetic  1.77 us (1%)
    psum x1, waiting for transfers between devices, body(): summed = lax.psum(within, 'grp')  44.7 us
    reduce_scatter x1, waiting for transfers between devices, body(): lax.psum_scatter(lax.dot_general(table, joined, (((0,), (0,)), ((), ())),...  32.2 us
    dot_general x1, matrix products, body(): lax.dot_general(waves[:, :atom_rows], waves, (((0,), (0,)), ((), ())), pr...  9.22 us
    ppermute x3, starting transfers between devices, shifted(): lax.ppermute(value, axis, [(i, (i + by) % size) for i in range(size)])  7.04 us
    all_gather x1, waiting for transfers between devices, body(): coeffs = lax.all_gather(coeffs, 'dev', axis=0, tiled=True)  5.78 us
    dot_general x1, matrix products, body(): forward = jnp.dot(weights, sources, preferred_element_type=jnp.float32)  5.5 us
    dot_general x1, matrix products, body(): long_range = jnp.dot(table, coeffs, preferred_element_type=jnp.float32)  4.49 us
    broadcast_in_dim x1, local copies, waits for them, and re-layouts, body(): jnp.repeat(jnp.repeat(times, TILE, axis=0), TILE, axis=1)  4.46 us
  transfers between devices with their start and end apart: 6, of which 3 were waited for; matrix products, arithmetic and copies ran while one was open for 19% of the time, Pallas kernels for 0%

profile of v1, /device:TPU:0, one launch (start us, length us, event | category | flops | bytes accessed | tf_op | source)
XLA Modules:
  0.0 144.0 jit_solution(12338820538972740979)
XLA Ops:
  7.2 0.0 copy-start
  7.2 0.0 copy-start.4
  7.2 0.0 reduce-scatter.2.cloned.1.call-start
  7.2 3.1 %fusion.2 = (bf16[1024,512]{0,1:T(8,128)(2,1)S(1)}, bf16[1024,512]{0,1:T(8,128)(2,1)S(1)}) fusion(bf16[3,1024]{1,0:T(4,128)(2,1)} %param.10, s32[3,512]{1,0:T(4,128)} %param.11), kind=kOutput, calls=%fused_computation.10 | convolution fusion | flops 19400192 | bytes 2109440 | tf_op jit(solution)/shard_map/dot_general | solution.py:29
  10.3 0.0 copy-start.6
  10.3 0.0 copy-start.7
  10.3 1.0 copy-done.6
  11.3 0.3 copy-done.7
  11.7 0.0 copy-done.4
  11.7 3.6 %fusion.8 = f32[1024,512]{1,0:T(8,128)} fusion(bf16[1024,512]{0,1:T(8,128)(2,1)S(1)} %get-tuple-element.5, bf16[1024,512]{0,1:T(8,128)(2,1)S(1)} %get-tuple-element.4, bf16[1024,256]{1,0:T(8,128)(2,1)S(1)} %copy-done.4, bf16[1024,256]{1,0:T(8,128)(2,1)} %param.8), kind=kOutput, calls=%fused_computation.21 | convolution fusion | flops 1080033280 | bytes 5242880 | tf_op jit(solution)/shard_map/dot_general | solution.py:48
  15.3 0.0 copy-start.2
  15.3 0.0 copy-start.3
  15.3 0.0 reduce-scatter.2.cloned.1.call-update
  15.4 0.0 all-reduce.2.cloned.1.call-start
  15.4 0.6 copy-done.2
  16.0 6.4 %collective-permute-start = (bf16[3,1024]{1,0:T(4,128)(2,1)S(1)}, bf16[3,1024]{1,0:T(4,128)(2,1)S(1)}, u32[]{:S(2)}, u32[]{:S(2)}) collective-permute-start(bf16[3,1024]{1,0:T(4,128)(2,1)S(1)} %copy-done.2), channel_id=1, source_target_pairs={{0,31},{1,0},{2,1},{3,2},{4,3},{5,4},{6,5},{7,6},{8,7},{9,8},{10,9... | collective-permute-start | bytes 18440 | tf_op jit(solution)/shard_map/ppermute | solution.py:14
  22.4 0.7 collective-permute-start.1
  23.7 0.0 copy-done
  23.7 32.2 %reduce-scatter.2.cloned.1.call-done = f32[128,512]{1,0:T(8,128)} async-done(((f32[1024,512]{1,0:T(8,128)}), f32[128,512]{1,0:T(8,128)}) %reduce-scatter.2.cloned.1.call-update) | async-done | bytes 262160 | tf_op jit(solution)/shard_map/reduce_scatter | solution.py:47
  56.0 0.0 all-reduce.2.cloned.1.call-update
  56.0 0.0 all-gather.2.cloned.1.call-start
  56.0 0.0 copy-done.3
  56.1 44.7 %all-reduce.2.cloned.1.call-done = f32[128,512]{1,0:T(8,128)} async-done(((f32[128,512]{1,0:T(8,128)}), f32[128,512]{1,0:T(8,128)}) %all-reduce.2.cloned.1.call-update) | async-done | bytes 262160 | tf_op jit(solution)/shard_map/psum | solution.py:51
  100.8 1.6 %fusion.23 = bf16[128,512]{1,0:T(8,128)(2,1)} fusion(f32[128,512]{1,0:T(8,128)} %all-reduce.2.cloned.1.call-done, f32[128,256]{1,0:T(8,128)S(1)} %constant_dynamic-slice_fusion), kind=kLoop, calls=%fused_computation.37 | loop fusion | flops 262144 | bytes 524288 | tf_op jit(solution)/shard_map/convert_element_type | solution.py:53
  102.4 0.0 all-gather.2.cloned.1.call-update
  102.4 0.2 convolution_convert_fusion.1
  102.7 0.0 collective-permute-done
  102.7 0.1 fusion.28
  102.8 0.1 multiply_multiply_fusion.6
  102.9 4.5 %broadcast_in_dim.10 = bf16[1024,16,128]{2,1,0:T(8,128)(2,1)S(1)} broadcast(bf16[1024,16]{1,0:T(8,128)(2,1)S(1)} %bitcast.18), dimensions={0,1} | broadcast | bytes 4227072 | tf_op jit(solution)/shard_map/broadcast_in_dim | solution.py:69
  107.3 9.2 %bitcast_multiply_fusion = bf16[1024,2048]{1,0:T(8,128)(2,1)S(1)} fusion(bf16[128,8,16,128]{3,2,1,0:T(8,128)(2,1)S(1)} %bitcast.17, f32[3,2048]{1,0:T(4,128)S(1)} %multiply_multiply_fusion.6, f32[3,2048]{1,0:T(4,128)S(1)} %get-tuple-element.2), kind=kOutput, calls=%fused_computation.1 | convolution fusion | flops 159401984 | bytes 8437760 | tf_op jit(solution)/shard_map/dot_general | solution.py:61
  116.6 0.0 copy-start.5
  116.6 1.4 fusion.47
  117.9 0.6 copy-done.5
  118.5 0.8 slice.42
  119.4 0.0 copy-start.1
  119.4 0.0 collective-permute-start.2
  119.4 5.8 %all-gather.2.cloned.1.call-done = bf16[1024,512]{1,0:T(8,128)(2,1)} async-done(((bf16[128,512]{1,0:T(8,128)(2,1)}), bf16[1024,512]{1,0:T(8,128)(2,1)}) %all-gather.2.cloned.1.call-update) | async-done | bytes 1048592 | tf_op jit(solution)/shard_map/all_gather | solution.py:54
  125.2 4.5 %fusion.7 = f32[1024,512]{1,0:T(8,128)} fusion(bf16[1024,512]{1,0:T(8,128)(2,1)} %all-gather.2.cloned.1.call-done, bf16[1024,512]{0,1:T(8,128)(2,1)} %copy-done.7, bf16[1024,512]{0,1:T(8,128)(2,1)} %copy-done.6), kind=kOutput, calls=%fused_computation.20 | convolution fusion | flops 1077936128 | bytes 5242880 | tf_op jit(solution)/shard_map/dot_general | solution.py:76
  129.6 0.0 collective-permute-done.1
  129.6 0.0 copy-done.1
  129.7 5.5 %fusion.9 = bf16[1024,256]{1,0:T(8,128)(2,1)} fusion(bf16[1024,2048]{1,0:T(8,128)(2,1)} %copy-done.5, bf16[256,256]{1,0:T(8,128)(2,1)S(1)} %copy-done.1, f32[1024,512]{1,0:T(8,128)} %fusion.7, bf16[1024,256]{1,0:T(8,128)(2,1)} %collective-permute-done.1, bf16[1024,256]{1,0:T(8,128)(2,1)} %param.8), kind=kOutput, calls=%fused_computation.23 | convolution fusion | flops 1345323008 | bytes 6946816 | tf_op jit(solution)/shard_map/dot_general | solution.py:71
  135.1 0.0 collective-permute-done.2
  135.2 2.4 %fusion.10 = bf16[1024,256]{1,0:T(8,128)(2,1)} fusion(bf16[256,256]{1,0:T(8,128)(2,1)S(1)} %copy-done.1, f32[1024,512]{1,0:T(8,128)} %fusion.7, f32[2048,256]{1,0:T(8,128)S(1)} %fusion.47, bf16[1024,256]{1,0:T(8,128)(2,1)S(1)} %collective-permute-done.2), kind=kOutput, calls=%fused_computation.24 | convolution fusion | flops 135528448 | bytes 3276800 | tf_op jit(solution)/shard_map/dot_general | solution.py:75
  (4 shorter events, 0.1 us)
Async XLA Ops:
  7.2 16.6 %copy-start = (f32[512,256]{1,0:T(8,128)S(1)}, f32[512,256]{1,0:T(8,128)}, u32[]{:S(2)}) copy-start(f32[512,256]{1,0:T(8,128)} %param.14) | copy-start | bytes 1572868
  7.2 4.5 %copy-start.4 = (bf16[1024,256]{1,0:T(8,128)(2,1)S(1)}, bf16[1024,256]{1,0:T(8,128)(2,1)}, u32[]{:S(2)}) copy-start(bf16[1024,256]{1,0:T(8,128)(2,1)} %param.9) | copy-start | bytes 1572868
  7.2 48.8 %reduce-scatter.2.cloned.1.call-start = ((), (), s32[]{:S(2)}) async-start(), calls=%async_computation.1 | async-start | bytes 2359296 | tf_op jit(solution)/shard_map/reduce_scatter | solution.py:47
  10.3 1.0 copy-start.6
  10.3 1.4 copy-start.7
  15.3 0.7 copy-start.2
  15.3 40.7 %copy-start.3 = (s32[24,2]{0,1:T(2,128)S(1)}, s32[24,2]{0,1:T(2,128)}, u32[]{:S(2)}) copy-start(s32[24,2]{0,1:T(2,128)} %param.12) | copy-start | bytes 580
  15.4 85.4 %all-reduce.2.cloned.1.call-start = ((), (), s32[]{:S(2)}) async-start(), calls=%async_computation.2 | async-start | bytes 524288 | tf_op jit(solution)/shard_map/psum | solution.py:51
  16.0 86.7 %collective-permute-start = (bf16[3,1024]{1,0:T(4,128)(2,1)S(1)}, bf16[3,1024]{1,0:T(4,128)(2,1)S(1)}, u32[]{:S(2)}, u32[]{:S(2)}) collective-permute-start(bf16[3,1024]{1,0:T(4,128)(2,1)S(1)} %copy-done.2), channel_id=1, source_target_pairs={{0,31},{1,0},{2,1},{3,2},{4,3},{5,4},{6,5},{7,6},{8,7},{9,8},{10,9... | collective-permute-start | bytes 18440 | tf_op jit(solution)/shard_map/ppermute | solution.py:14
  22.4 107.3 %collective-permute-start.1 = (bf16[1024,256]{1,0:T(8,128)(2,1)}, bf16[1024,256]{1,0:T(8,128)(2,1)}, u32[]{:S(2)}, u32[]{:S(2)}) collective-permute-start(bf16[1024,256]{1,0:T(8,128)(2,1)} %param.8), channel_id=1, source_target_pairs={{0,31},{1,0},{2,1},{3,2},{4,3},{5,4},{6,5},{7,6},{8,7},{9,8},{10,9... | collective-permute-start | bytes 1572872 | tf_op jit(solution)/shard_map/ppermute | solution.py:14
  56.0 69.2 %all-gather.2.cloned.1.call-start = ((), (), s32[]{:S(2)}) async-start(), calls=%async_computation.3 | async-start | bytes 1179648 | tf_op jit(solution)/shard_map/all_gather | solution.py:54
  116.6 2.0 %copy-start.5 = (bf16[1024,2048]{1,0:T(8,128)(2,1)}, bf16[1024,2048]{1,0:T(8,128)(2,1)S(1)}, u32[]{:S(2)}) copy-start(bf16[1024,2048]{1,0:T(8,128)(2,1)S(1)} %bitcast_multiply_fusion) | copy-start | bytes 12582916
  119.4 10.3 %copy-start.1 = (bf16[256,256]{1,0:T(8,128)(2,1)S(1)}, bf16[256,256]{1,0:T(8,128)(2,1)}, u32[]{:S(2)}) copy-start(bf16[256,256]{1,0:T(8,128)(2,1)} %param.15) | copy-start | bytes 393220
  119.4 15.8 %collective-permute-start.2 = (bf16[1024,256]{1,0:T(8,128)(2,1)}, bf16[1024,256]{1,0:T(8,128)(2,1)S(1)}, u32[]{:S(2)}, u32[]{:S(2)}) collective-permute-start(bf16[1024,256]{1,0:T(8,128)(2,1)} %slice.42), channel_id=1, source_target_pairs={{0,1},{1,2},{2,3},{3,4},{4,5},{5,6},{6,7},{7,8},{8,9},{9,10},{10,1... | collective-permute-start | bytes 1572872 | tf_op jit(solution)/shard_map/ppermute | solution.py:14
Sparse Core Ops, SparseCore 0:
  15.5 40.4 reduce-scatter.1
  58.9 41.8 all-reduce.1
  103.0 22.0 all-gather.1

commit v2 on v1

--- a/solution.py
+++ b/solution.py
@@ -1,8 +1,11 @@
+import functools
 import math
 
 import jax
 import jax.numpy as jnp
 from jax import lax
+from jax.experimental import pallas as pl
+from jax.experimental.pallas import tpu as pltpu
 from jax.sharding import PartitionSpec as P
 
 TILE = 128
@@ -33,9 +36,111 @@
     return jnp.concatenate([cosine.astype(jnp.bfloat16), sine.astype(jnp.bfloat16)], axis=1)
 
 
+def reduce_kernel(groups, depth, inv_root, part_ref, filter_ref, out_ref, half_in, half_sum, group_in, group_sum, depth_in, send_sem, recv_sem):
+    grp, dev = lax.axis_index("grp"), lax.axis_index("dev")
+    place, core = dev // 2, dev % 2
+    half = part_ref.shape[0] // 2
+    rows = half // groups
+    share = rows // depth
+    scatter = rows % depth == 0 and share % 16 == 0
+    other = {"dev": place * 2 + 1 - core}
+    group_peers = [lax.rem(grp + s, groups) for s in range(1, groups)]
+    place_peers = [lax.rem(place + s, depth) for s in range(1, depth)]
+    group_ids = [{"grp": p} for p in group_peers]
+    place_ids = [{"dev": p * 2 + core} for p in place_peers]
+    used = [0]
+
+    barrier = pltpu.get_barrier_semaphore()
+    for who in [other, *group_ids, *place_ids]:
+        pl.semaphore_signal(barrier, inc=1, device_id=who, device_id_type=pl.DeviceIdType.MESH)
+    pl.semaphore_wait(barrier, 1 + len(group_ids) + len(place_ids))
+
+    def span(start, size):
+        return pl.ds(pl.multiple_of(start, 16), size)
+
+    def exchange(moves):
+        copies = []
+        for source, target, who in moves:
+            copies.append(pltpu.make_async_remote_copy(
+                src_ref=source, dst_ref=target, send_sem=send_sem.at[used[0]], recv_sem=recv_sem.at[used[0]],
+                device_id=who, device_id_type=pl.DeviceIdType.MESH,
+            ))
+            used[0] += 1
+        for copy in copies:
+            copy.start()
+        for copy in copies:
+            copy.wait()
+
+    def filtered(total, start):
+        gain = filter_ref[span(start, total.shape[0]), :]
+        return (total * jnp.concatenate([gain, gain], axis=1) * inv_root).astype(jnp.bfloat16)
+
+    exchange([(part_ref.at[span((1 - core) * half, half)], half_in, other)])
+    half_sum[...] = (
+        part_ref[span(core * half, half), :].astype(jnp.float32) + half_in[...].astype(jnp.float32)
+    ).astype(jnp.bfloat16)
+
+    exchange([
+        (half_sum.at[span(p * rows, rows)], group_in.at[s], who)
+        for s, (p, who) in enumerate(zip(group_peers, group_ids))
+    ])
+    total = half_sum[span(grp * rows, rows), :].astype(jnp.float32)
+    for s in range(groups - 1):
+        total = total + group_in[s].astype(jnp.float32)
+    group_sum[...] = total.astype(jnp.bfloat16)
+
+    base = core * half + grp * rows
+    if scatter:
+        exchange([
+            (group_sum.at[span(p * share, share)], depth_in.at[s], who)
+            for s, (p, who) in enumerate(zip(place_peers, place_ids))
+        ])
+        total = group_sum[span(place * share, share), :].astype(jnp.float32)
+        for s in range(depth - 1):
+            total = total + depth_in[s].astype(jnp.float32)
+        mine = span(base + place * share, share)
+        out_ref[mine, :] = filtered(total, grp * rows + place * share)
+        exchange([(out_ref.at[mine], out_ref.at[mine], who) for who in place_ids])
+    else:
+        exchange([(group_sum, depth_in.at[s], who) for s, who in enumerate(place_ids)])
+        total = group_sum[...].astype(jnp.float32)
+        for s in range(depth - 1):
+            total = total + depth_in[s].astype(jnp.float32)
+        out_ref[span(base, rows), :] = filtered(total, grp * rows)
+    mine = span(base, rows)
+    exchange([(out_ref.at[mine], out_ref.at[mine], who) for who in group_ids])
+    mine = span(core * half, half)
+    exchange([(out_ref.at[mine], out_ref.at[mine], other)])
+
+
+def reduced(part, wave_filter, inv_root):
+    groups, depth = lax.axis_size("grp"), lax.axis_size("dev") // 2
+    total_rows, width = part.shape
+    half = total_rows // 2
+    rows = half // groups
+    share = rows // depth if rows % depth == 0 and (rows // depth) % 16 == 0 else rows
+    copies = 2 + 2 * (groups - 1) + 2 * (depth - 1)
+    return pl.pallas_call(
+        functools.partial(reduce_kernel, groups, depth, inv_root),
+        out_shape=jax.ShapeDtypeStruct(part.shape, jnp.bfloat16),
+        in_specs=[pl.BlockSpec(memory_space=pltpu.VMEM)] * 2,
+        out_specs=pl.BlockSpec(memory_space=pltpu.VMEM),
+        scratch_shapes=[
+            pltpu.VMEM((half, width), jnp.bfloat16),
+            pltpu.VMEM((half, width), jnp.bfloat16),
+            pltpu.VMEM((groups - 1, rows, width), jnp.bfloat16),
+            pltpu.VMEM((rows, width), jnp.bfloat16),
+            pltpu.VMEM((depth - 1, share, width), jnp.bfloat16),
+            pltpu.SemaphoreType.DMA((copies,)),
+            pltpu.SemaphoreType.DMA((copies,)),
+        ],
+        compiler_params=pltpu.CompilerParams(collective_id=0, has_side_effects=True, vmem_limit_bytes=16 * 2**20),
+        cost_estimate=pl.CostEstimate(flops=4 * part.size, bytes_accessed=8 * part.size, transcendentals=0),
+    )(part, wave_filter)
+
+
 def body(embedding, cotangent, fractional, wave_index, tile_pairs, counts, wave_filter, short_weight):
     atom_rows, channels = embedding.shape
-    wave_count = wave_index.shape[1]
     tiles = atom_rows // TILE
     pair_rows = tile_pairs.shape[0]
     blocks = lax.axis_size("grp") * lax.axis_size("dev")
@@ -43,15 +148,8 @@
     above_embedding, above_places = shifted((embedding, fractional), ("grp", "dev"), -1)
     table = trig_table(fractional, wave_index)
     joined = jnp.concatenate([embedding, cotangent], axis=1)
-    rows = 2 * wave_count // lax.axis_size("dev")
-    within = lax.psum_scatter(
-        lax.dot_general(table, joined, (((0,), (0,)), ((), ())), preferred_element_type=jnp.float32),
-        "dev", scatter_dimension=0, tiled=True,
-    )
-    summed = lax.psum(within, "grp")
-    local = lax.dynamic_slice_in_dim(wave_filter, lax.axis_index("dev") * rows % wave_count, rows, 0)
-    coeffs = (summed * jnp.concatenate([local, local], axis=1) * inv_root).astype(jnp.bfloat16)
-    coeffs = lax.all_gather(coeffs, "dev", axis=0, tiled=True)
+    part = lax.dot_general(table, joined, (((0,), (0,)), ((), ())), preferred_element_type=jnp.float32)
+    coeffs = reduced(part.astype(jnp.bfloat16), wave_filter, inv_root)
 
     sources = jnp.dot(
         jnp.concatenate([embedding, above_embedding], axis=0), short_weight, preferred_element_type=jnp.float32

time: 144 us -> 71.9 us (0.50)
  waiting for transfers between devices: 82.7 us -> 3.73 us
  Pallas kernels: 0 us -> 27.1 us
  between operations: 14.5 us -> 1.42 us
  matrix products: 29.9 us -> 25.6 us
  local copies, waits for them, and re-layouts: 7.96 us -> 5.93 us
  other arithmetic: 1.77 us -> 0.13 us
    psum x1 -> x0, waiting for transfers between devices: 44.7 us -> none  [body(): summed = lax.psum(within, 'grp')]
    reduce_scatter x1 -> x0, waiting for transfers between devices: 32.2 us -> none  [body(): lax.psum_scatter(lax.dot_general(table, joined, (((0,), (0,)), ((), ())),...]
    pallas_call x0 -> x1, Pallas kernels: none -> 27.1 us  [reduced(): pl.pallas_call(functools.partial(reduce_kernel, groups, depth, inv_root),...]
    all_gather x1 -> x0, waiting for transfers between devices: 5.78 us -> none  [body(): coeffs = lax.all_gather(coeffs, 'dev', axis=0, tiled=True)]
    ppermute x3, waiting for transfers between devices: 0.01 us -> 3.73 us  [shifted(): lax.ppermute(value, axis, [(i, (i + by) % size) for i in range(size)])]
    dot_general x1, matrix products: 3.64 us -> 1.26 us  [body(): lax.dot_general(table, joined, (((0,), (0,)), ((), ())), preferred_elemen...]
    unnamed x16 -> x12, local copies, waits for them, and re-layouts: 2.59 us -> 0.62 us
    dot_general x1, matrix products: 4.49 us -> 2.6 us  [body(): long_range = jnp.dot(table, coeffs, preferred_element_type=jnp.float32)]
  transfers between devices with their start and end apart: 6 -> 3, of which waited for: 3 -> 1; matrix products, arithmetic and copies ran while one was open for 19% -> 40% of each run, Pallas kernels for 0% -> 38%
where the time goes in v2:
time: 71.9 us; the launch traced here: 71.6 us
  Pallas kernels  27.1 us (38%)
  matrix products  25.6 us (36%)
  starting transfers between devices  7.7 us (11%)
  local copies, waits for them, and re-layouts  5.93 us (8%)
  waiting for transfers between devices  3.73 us (5%)
  between operations  1.42 us (2%)
    pallas_call x1, Pallas kernels, reduced(): pl.pallas_call(functools.partial(reduce_kernel, groups, depth, inv_root),...  27.1 us
    dot_general x1, matrix products, body(): lax.dot_general(waves[:, :atom_rows], waves, (((0,), (0,)), ((), ())), pr...  9.22 us
    ppermute x3, starting transfers between devices, shifted(): lax.ppermute(value, axis, [(i, (i + by) % size) for i in range(size)])  7.7 us
    dot_general x1, matrix products, body(): forward = jnp.dot(weights, sources, preferred_element_type=jnp.float32)  5.5 us
    broadcast_in_dim x1, local copies, waits for them, and re-layouts, body(): jnp.repeat(jnp.repeat(times, TILE, axis=0), TILE, axis=1)  4.46 us
    ppermute x3, waiting for transfers between devices, shifted(): lax.ppermute(value, axis, [(i, (i + by) % size) for i in range(size)])  3.73 us
    dot_general x1, matrix products, trig_table(): lax.dot_general(places, wave_index.astype(jnp.bfloat16), (((0,), (0,)), (...  3.06 us
    dot_general x1, matrix products, body(): long_range = jnp.dot(table, coeffs, preferred_element_type=jnp.float32)  2.6 us
  transfers between devices with their start and end apart: 3, of which 1 were waited for; matrix products, arithmetic and copies ran while one was open for 40% of the time, Pallas kernels for 38%

profile of v2, /device:TPU:0, one launch (start us, length us, event | category | flops | bytes accessed | tf_op | source)
XLA Modules:
  0.0 71.6 jit_solution(16809524229572648650)
XLA Ops:
  0.6 0.0 copy-start
  0.6 6.4 %collective-permute-start = (bf16[3,1024]{1,0:T(4,128)(2,1)}, bf16[3,1024]{1,0:T(4,128)(2,1)S(1)}, u32[]{:S(2)}, u32[]{:S(2)}) collective-permute-start(bf16[3,1024]{1,0:T(4,128)(2,1)} %param.10), channel_id=1, source_target_pairs={{0,31},{1,0},{2,1},{3,2},{4,3},{5,4},{6,5},{7,6},{8,7},{9,8},{10,9... | collective-permute-start | bytes 18440 | tf_op jit(solution)/shard_map/ppermute | solution.py:17
  7.1 0.7 collective-permute-start.1
  7.7 0.8 %slice_bitcast_fusion.1 = (s32[24]{0:T(128)S(1)}, s32[24]{0:T(128)S(1)}) fusion(s32[24,2]{0,1:T(2,128)} %param.12), kind=kLoop, calls=%fused_computation.65 | loop fusion | bytes 384 | tf_op jit(solution)/shard_map/eq | solution.py:163
  9.2 0.0 copy-start.3
  9.2 0.0 copy-start.4
  9.2 3.1 %fusion.2 = (bf16[1024,512]{0,1:T(8,128)(2,1)S(1)}, bf16[1024,512]{0,1:T(8,128)(2,1)S(1)}) fusion(bf16[3,1024]{1,0:T(4,128)(2,1)} %param.10, s32[3,512]{1,0:T(4,128)} %param.11), kind=kOutput, calls=%fused_computation.10 | convolution fusion | flops 19400192 | bytes 2109440 | tf_op jit(solution)/shard_map/dot_general | solution.py:32
  12.3 0.2 convolution_convert_fusion.2
  12.5 0.0 copy-done.3
  12.5 0.0 copy-done.4
  12.5 0.0 copy-start.1
  12.5 1.3 %convolution_convert_fusion.1.part_ref = bf16[1024,512]{1,0:T(8,128)(2,1)S(1)} fusion(bf16[1024,512]{0,1:T(8,128)(2,1)S(1)} %get-tuple-element.5, bf16[1024,512]{0,1:T(8,128)(2,1)S(1)} %get-tuple-element.4, bf16[1024,256]{1,0:T(8,128)(2,1)S(1)} %copy-done.3, bf16[1024,256]{1,0:T(8,128)(2,1)S(1)} %copy-done.4), kind=kOutput, calls=%fused_computation.19 | convolution fusion | flops 1080557568 | bytes 4194304 | tf_op jit(solution)/shard_map/dot_general | solution.py:151
  13.8 0.0 copy-done.1
  13.8 0.0 copy-start.2
  13.8 27.1 %shard_map.95 = bf16[1024,512]{1,0:T(8,128)(2,1)S(1)} custom-call(bf16[1024,512]{1,0:T(8,128)(2,1)S(1)} %convolution_convert_fusion.1.part_ref, f32[512,256]{1,0:T(8,128)S(1)} %copy-done.1), custom_call_target="tpu_custom_call" | custom-call | flops 2097152 | bytes 4194304 | tf_op jit(solution)/shard_map/pallas_call | solution.py:123
  40.9 0.0 collective-permute-done
  40.9 0.0 copy-done.2
  40.9 0.1 fusion.25
  41.0 0.1 multiply_multiply_fusion.6
  41.1 4.5 %broadcast_in_dim.10 = bf16[1024,16,128]{2,1,0:T(8,128)(2,1)S(1)} broadcast(bf16[1024,16]{1,0:T(8,128)(2,1)S(1)} %bitcast.18), dimensions={0,1} | broadcast | bytes 4227072 | tf_op jit(solution)/shard_map/broadcast_in_dim | solution.py:167
  45.6 9.2 %bitcast_multiply_fusion = bf16[1024,2048]{1,0:T(8,128)(2,1)S(1)} fusion(bf16[128,8,16,128]{3,2,1,0:T(8,128)(2,1)S(1)} %bitcast.17, f32[3,2048]{1,0:T(4,128)S(1)} %multiply_multiply_fusion.6, f32[3,2048]{1,0:T(4,128)S(1)} %get-tuple-element.2), kind=kOutput, calls=%fused_computation.1 | convolution fusion | flops 159401984 | bytes 8437760 | tf_op jit(solution)/shard_map/dot_general | solution.py:159
  54.8 0.0 copy-start.5
  54.8 1.4 %fusion.44 = f32[2048,256]{1,0:T(8,128)S(1)} fusion(bf16[1024,2048]{1,0:T(8,128)(2,1)S(1)} %bitcast_multiply_fusion, bf16[1024,256]{1,0:T(8,128)(2,1)S(1)} %copy-done.3), kind=kOutput, calls=%fused_computation.70 | convolution fusion | flops 1073741824 | bytes 6815744 | tf_op jit(solution)/shard_map/dot_general | solution.py:170
  56.2 0.6 copy-done.5
  56.8 0.1 slice.42
  56.8 0.6 collective-permute-start.2
  57.4 2.6 %fusion.7 = f32[1024,512]{1,0:T(8,128)} fusion(bf16[1024,512]{1,0:T(8,128)(2,1)S(1)} %shard_map.95, bf16[1024,512]{0,1:T(8,128)(2,1)S(1)} %get-tuple-element.5, bf16[1024,512]{0,1:T(8,128)(2,1)S(1)} %get-tuple-element.4), kind=kOutput, calls=%fused_computation.21 | convolution fusion | flops 1077936128 | bytes 5242880 | tf_op jit(solution)/shard_map/dot_general | solution.py:174
  60.0 0.0 collective-permute-done.1
  60.0 0.0 copy-done
  60.1 5.5 %fusion.8 = bf16[1024,256]{1,0:T(8,128)(2,1)} fusion(bf16[1024,2048]{1,0:T(8,128)(2,1)} %copy-done.5, bf16[256,256]{1,0:T(8,128)(2,1)S(1)} %copy-done, f32[1024,512]{1,0:T(8,128)} %fusion.7, bf16[1024,256]{1,0:T(8,128)(2,1)} %collective-permute-done.1, bf16[1024,256]{1,0:T(8,128)(2,1)} %param.8), kind=kOutput, calls=%fused_computation.23 | convolution fusion | flops 1345323008 | bytes 6946816 | tf_op jit(solution)/shard_map/dot_general | solution.py:169
  65.5 3.7 %collective-permute-done.2 = bf16[1024,256]{1,0:T(8,128)(2,1)S(1)} collective-permute-done((bf16[1024,256]{1,0:T(8,128)(2,1)S(1)}, bf16[1024,256]{1,0:T(8,128)(2,1)S(1)}, u32[]{:S(2)}, u32[]{:S(2)}) %collective-permute-start.2) | collective-permute-done | bytes 524320 | tf_op jit(solution)/shard_map/ppermute | solution.py:17
  69.3 2.4 %fusion.9 = bf16[1024,256]{1,0:T(8,128)(2,1)} fusion(bf16[256,256]{1,0:T(8,128)(2,1)S(1)} %copy-done, f32[1024,512]{1,0:T(8,128)} %fusion.7, f32[2048,256]{1,0:T(8,128)S(1)} %fusion.44, bf16[1024,256]{1,0:T(8,128)(2,1)S(1)} %collective-permute-done.2), kind=kOutput, calls=%fused_computation.24 | convolution fusion | flops 135528448 | bytes 3276800 | tf_op jit(solution)/shard_map/dot_general | solution.py:173
  (2 shorter events, 0.0 us)
Async XLA Ops:
  0.6 59.4 %copy-start = (bf16[256,256]{1,0:T(8,128)(2,1)S(1)}, bf16[256,256]{1,0:T(8,128)(2,1)}, u32[]{:S(2)}) copy-start(bf16[256,256]{1,0:T(8,128)(2,1)} %param.15) | copy-start | bytes 393220
  0.6 40.3 %collective-permute-start = (bf16[3,1024]{1,0:T(4,128)(2,1)}, bf16[3,1024]{1,0:T(4,128)(2,1)S(1)}, u32[]{:S(2)}, u32[]{:S(2)}) collective-permute-start(bf16[3,1024]{1,0:T(4,128)(2,1)} %param.10), channel_id=1, source_target_pairs={{0,31},{1,0},{2,1},{3,2},{4,3},{5,4},{6,5},{7,6},{8,7},{9,8},{10,9... | collective-permute-start | bytes 18440 | tf_op jit(solution)/shard_map/ppermute | solution.py:17
  7.1 53.0 %collective-permute-start.1 = (bf16[1024,256]{1,0:T(8,128)(2,1)}, bf16[1024,256]{1,0:T(8,128)(2,1)}, u32[]{:S(2)}, u32[]{:S(2)}) collective-permute-start(bf16[1024,256]{1,0:T(8,128)(2,1)} %param.8), channel_id=1, source_target_pairs={{0,31},{1,0},{2,1},{3,2},{4,3},{5,4},{6,5},{7,6},{8,7},{9,8},{10,9... | collective-permute-start | bytes 1572872 | tf_op jit(solution)/shard_map/ppermute | solution.py:17
  9.2 3.3 %copy-start.3 = (bf16[1024,256]{1,0:T(8,128)(2,1)S(1)}, bf16[1024,256]{1,0:T(8,128)(2,1)}, u32[]{:S(2)}) copy-start(bf16[1024,256]{1,0:T(8,128)(2,1)} %param.9) | copy-start | bytes 1572868
  9.2 3.3 %copy-start.4 = (bf16[1024,256]{1,0:T(8,128)(2,1)S(1)}, bf16[1024,256]{1,0:T(8,128)(2,1)}, u32[]{:S(2)}) copy-start(bf16[1024,256]{1,0:T(8,128)(2,1)} %param.8) | copy-start | bytes 1572868
  12.5 1.3 %copy-start.1 = (f32[512,256]{1,0:T(8,128)S(1)}, f32[512,256]{1,0:T(8,128)}, u32[]{:S(2)}) copy-start(f32[512,256]{1,0:T(8,128)} %filter_ref.1) | copy-start | bytes 1572868
  13.8 27.1 %copy-start.2 = (bf16[3,1024]{1,0:T(4,128)(2,1)S(1)}, bf16[3,1024]{1,0:T(4,128)(2,1)}, u32[]{:S(2)}) copy-start(bf16[3,1024]{1,0:T(4,128)(2,1)} %param.10) | copy-start | bytes 18436
  54.8 2.0 %copy-start.5 = (bf16[1024,2048]{1,0:T(8,128)(2,1)}, bf16[1024,2048]{1,0:T(8,128)(2,1)S(1)}, u32[]{:S(2)}) copy-start(bf16[1024,2048]{1,0:T(8,128)(2,1)S(1)} %bitcast_multiply_fusion) | copy-start | bytes 12582916
  56.8 12.4 %collective-permute-start.2 = (bf16[1024,256]{1,0:T(8,128)(2,1)S(1)}, bf16[1024,256]{1,0:T(8,128)(2,1)S(1)}, u32[]{:S(2)}, u32[]{:S(2)}) collective-permute-start(bf16[1024,256]{1,0:T(8,128)(2,1)S(1)} %slice.42), channel_id=1, source_target_pairs={{0,1},{1,2},{2,3},{3,4},{4,5},{5,6},{6,7},{7,8},{8,9},{9,10},{10,1... | collective-permute-start | bytes 1572872 | tf_op jit(solution)/shard_map/ppermute | solution.py:17

commit v3 on v2

v3 whole, which is shorter than its diff:
```python
import functools
import math

import jax
import jax.numpy as jnp
from jax import lax
from jax.experimental import pallas as pl
from jax.experimental.pallas import tpu as pltpu
from jax.sharding import PartitionSpec as P

TILE = 128
two_pi = 2.0 * math.pi


def shifted(value, axis, by):
    size = lax.axis_size(axis)
    return lax.ppermute(value, axis, [(i, (i + by) % size) for i in range(size)])


def cos_sin(turns):
    rest = turns - jnp.round(turns)
    angle = rest * (two_pi / 4.0)
    sq = angle * angle
    sine = angle * (1.0 + sq * (-1.0 / 6 + sq * (1.0 / 120 + sq * (-1.0 / 5040 + sq * (1.0 / 362880)))))
    cosine = 1.0 + sq * (-0.5 + sq * (1.0 / 24 + sq * (-1.0 / 720 + sq * (1.0 / 40320))))
    for _ in range(2):
        sine, cosine = 2.0 * sine * cosine, 1.0 - 2.0 * sine * sine
    return cosine, sine


def trig_table(places, wave_index):
    turns = lax.dot_general(
        places, wave_index.astype(jnp.bfloat16), (((0,), (0,)), ((), ())), preferred_element_type=jnp.float32
    )
    cosine, sine = cos_sin(turns)
    return jnp.concatenate([cosine.astype(jnp.bfloat16), sine.astype(jnp.bfloat16)], axis=1)


def reduce_kernel(groups, depth, inv_root, part_ref, sent_ref, filter_ref, left_ref, right_ref, times_ref, sources_ref, cot_ref,
                  out_ref, forward_ref, grad_ref, half_wide, half_in, half_sum, group_wide, group_in, group_sum, depth_in,
                  backward, back_out, back_in, send_sem, recv_sem):
    grp, dev = lax.axis_index("grp"), lax.axis_index("dev")
    place, core = dev // 2, dev % 2
    half = part_ref.shape[0] // 2
    rows = half // groups
    share = rows // depth
    scatter = rows % depth == 0 and share % 16 == 0
    other = {"dev": place * 2 + 1 - core}
    group_peers = [lax.rem(grp + s, groups) for s in range(1, groups)]
    place_peers = [lax.rem(place + s, depth) for s in range(1, depth)]
    group_ids = [{"grp": p} for p in group_peers]
    place_ids = [{"dev": p * 2 + core} for p in place_peers]
    used = [0]

    barrier = pltpu.get_barrier_semaphore()
    devices = lax.axis_size("dev")
    blocks = groups * devices
    after, before = (lax.rem(grp * devices + dev + step, blocks) for step in (1, blocks - 1))
    next_id, last_id = ({"grp": b // devices, "dev": lax.rem(b, devices)} for b in (after, before))
    for who in [other, *group_ids, *place_ids, next_id, last_id]:
        pl.semaphore_signal(barrier, inc=1, device_id=who, device_id_type=pl.DeviceIdType.MESH)
    pl.semaphore_wait(barrier, 3 + len(group_ids) + len(place_ids))
    atom_rows = cot_ref.shape[0]
    tiles = atom_rows // TILE
    backward[...] = jnp.zeros_like(backward)

    def near_tile(u, carry):
        here = span(u * TILE, TILE)
        closeness = jnp.dot(left_ref[here, :], right_ref[...], preferred_element_type=jnp.float32)
        spread = (jnp.exp(closeness - 3.0) * (1.0 / math.sqrt(TILE))).astype(jnp.bfloat16)
        weights = (spread.astype(jnp.float32) * times_ref[pl.ds(u, 1), :]).astype(jnp.bfloat16)
        forward_ref[here, :] = jnp.dot(weights, sources_ref[...], preferred_element_type=jnp.float32)
        backward[...] += lax.dot_general(
            weights, cot_ref[here, :], (((0,), (0,)), ((), ())), preferred_element_type=jnp.float32
        )
        return carry

    def span(start, size):
        return pl.ds(pl.multiple_of(start, 16), size)

    def exchange(moves, first=0, last=0):
        copies = []
        for source, target, who in moves:
            copies.append(pltpu.make_async_remote_copy(
                src_ref=source, dst_ref=target, send_sem=send_sem.at[used[0]], recv_sem=recv_sem.at[used[0]],
                device_id=who, device_id_type=pl.DeviceIdType.MESH,
            ))
            used[0] += 1
        for copy in copies:
            copy.start()
        if last > first:
            lax.fori_loop(first, last, near_tile, 0)
        for copy in copies:
            copy.wait()

    def filtered(total, start):
        gain = filter_ref[span(start, total.shape[0]), :]
        return (total * jnp.concatenate([gain, gain], axis=1) * inv_root).astype(jnp.bfloat16)

    exchange([(sent_ref.at[span((1 - core) * half, half)], half_in, other)], 0, tiles // 8)
    half_wide[...] = part_ref[span(core * half, half), :] + half_in[...].astype(jnp.float32)
    half_sum[...] = half_wide[...].astype(jnp.bfloat16)

    exchange([
        (half_sum.at[span(p * rows, rows)], group_in.at[s], who)
        for s, (p, who) in enumerate(zip(group_peers, group_ids))
    ], tiles // 8, tiles // 2)
    total = half_wide[span(grp * rows, rows), :]
    for s in range(groups - 1):
        total = total + group_in[s].astype(jnp.float32)
    group_wide[...] = total
    group_sum[...] = total.astype(jnp.bfloat16)

    base = core * half + grp * rows
    if scatter:
        exchange([
            (group_sum.at[span(p * share, share)], depth_in.at[s], who)
            for s, (p, who) in enumerate(zip(place_peers, place_ids))
        ], tiles // 2, tiles * 3 // 4)
        total = group_wide[span(place * share, share), :]
        for s in range(depth - 1):
            total = total + depth_in[s].astype(jnp.float32)
        mine = span(base + place * share, share)
        out_ref[mine, :] = filtered(total, grp * rows + place * share)
        exchange([(out_ref.at[mine], out_ref.at[mine], who) for who in place_ids], tiles * 3 // 4, tiles)
    else:
        exchange([(group_sum, depth_in.at[s], who) for s, who in enumerate(place_ids)], tiles // 2, tiles)
        total = group_wide[...]
        for s in range(depth - 1):
            total = total + depth_in[s].astype(jnp.float32)
        out_ref[span(base, rows), :] = filtered(total, grp * rows)
    back_out[...] = backward[atom_rows:, :].astype(jnp.bfloat16)
    back = pltpu.make_async_remote_copy(
        src_ref=back_out, dst_ref=back_in, send_sem=send_sem.at[used[0]], recv_sem=recv_sem.at[used[0]],
        device_id=next_id, device_id_type=pl.DeviceIdType.MESH,
    )
    used[0] += 1
    back.start()
    mine = span(base, rows)
    exchange([(out_ref.at[mine], out_ref.at[mine], who) for who in group_ids])
    mine = span(core * half, half)
    exchange([(out_ref.at[mine], out_ref.at[mine], other)])
    back.wait()
    grad_ref[...] = (backward[:atom_rows, :] + back_in[...].astype(jnp.float32)).astype(jnp.bfloat16)


def reduced(part, wave_filter, left, right, times, sources, cotangent, inv_root):
    groups, depth = lax.axis_size("grp"), lax.axis_size("dev") // 2
    total_rows, width = part.shape
    half = total_rows // 2
    rows = half // groups
    share = rows // depth if rows % depth == 0 and (rows // depth) % 16 == 0 else rows
    copies = 3 + 2 * (groups - 1) + 2 * (depth - 1)
    return pl.pallas_call(
        functools.partial(reduce_kernel, groups, depth, inv_root),
        out_shape=(
            jax.ShapeDtypeStruct(part.shape, jnp.bfloat16),
            jax.ShapeDtypeStruct(cotangent.shape, jnp.float32),
            jax.ShapeDtypeStruct(cotangent.shape, jnp.bfloat16),
        ),
        in_specs=[pl.BlockSpec(memory_space=pltpu.VMEM)] * 8,
        out_specs=(pl.BlockSpec(memory_space=pltpu.VMEM),) * 3,
        scratch_shapes=[
            pltpu.VMEM((half, width), jnp.float32),
            pltpu.VMEM((half, width), jnp.bfloat16),
            pltpu.VMEM((half, width), jnp.bfloat16),
            pltpu.VMEM((rows, width), jnp.float32),
            pltpu.VMEM((groups - 1, rows, width), jnp.bfloat16),
            pltpu.VMEM((rows, width), jnp.bfloat16),
            pltpu.VMEM((depth - 1, share, width), jnp.bfloat16),
            pltpu.VMEM(sources.shape, jnp.float32),
            pltpu.VMEM(cotangent.shape, jnp.bfloat16),
            pltpu.VMEM(cotangent.shape, jnp.bfloat16),
            pltpu.SemaphoreType.DMA((copies,)),
            pltpu.SemaphoreType.DMA((copies,)),
        ],
        compiler_params=pltpu.CompilerParams(collective_id=0, has_side_effects=True, vmem_limit_bytes=40 * 2**20),
        cost_estimate=pl.CostEstimate(flops=4 * part.size, bytes_accessed=8 * part.size, transcendentals=0),
    )(part, part.astype(jnp.bfloat16), wave_filter, left, right, times, sources, cotangent)


def body(embedding, cotangent, fractional, wave_index, tile_pairs, counts, wave_filter, short_weight):
    atom_rows, channels = embedding.shape
    tiles = atom_rows // TILE
    pair_rows = tile_pairs.shape[0]
    blocks = lax.axis_size("grp") * lax.axis_size("dev")
    inv_root = 1.0 / math.sqrt(atom_rows * blocks)
    above_embedding, above_places = shifted((embedding, fractional), ("grp", "dev"), -1)
    table = trig_table(fractional, wave_index)
    joined = jnp.concatenate([embedding, cotangent], axis=1)
    part = lax.dot_general(table, joined, (((0,), (0,)), ((), ())), preferred_element_type=jnp.float32)

    sources = jnp.dot(
        jnp.concatenate([embedding, above_embedding], axis=0), short_weight, preferred_element_type=jnp.float32
    ).astype(jnp.bfloat16)
    cosine, sine = cos_sin(jnp.concatenate([fractional, above_places], axis=1).astype(jnp.float32))
    waves = jnp.concatenate([cosine, sine], axis=0)
    high = lax.reduce_precision(waves, 8, 7)
    low = (waves - high).astype(jnp.bfloat16)
    high = high.astype(jnp.bfloat16)
    left = jnp.concatenate([high, high, low], axis=0)[:, :atom_rows].T
    right = jnp.concatenate([high, low, high], axis=0)
    live = (jnp.arange(pair_rows, dtype=jnp.int32) < counts[0])[:, None]
    first_hot = ((tile_pairs[:, :1] == jnp.arange(tiles, dtype=jnp.int32)) & live).astype(jnp.float32)
    second_hot = (tile_pairs[:, 1:] == jnp.arange(2 * tiles, dtype=jnp.int32)).astype(jnp.float32)
    times = jnp.einsum("pu,pv->uv", first_hot, second_hot)
    times = jnp.repeat(times, TILE, axis=1)
    coeffs, forward, near_grad = reduced(part, wave_filter, left, right, times, sources, cotangent, inv_root)
    mixed = lax.dot_general(near_grad, short_weight, (((1,), (1,)), ((), ())), preferred_element_type=jnp.float32)
    long_range = jnp.dot(table, coeffs, preferred_element_type=jnp.float32)
    message = (long_range[:, :channels] + forward).astype(jnp.bfloat16)
    embedding_grad = (long_range[:, channels:] + mixed).astype(jnp.bfloat16)
    return (message, embedding_grad)


def solution(mesh):
    split = P(("grp", "dev"), None)
    in_specs = (split, split, P(None, ("grp", "dev")), P(), split, P(("grp", "dev")), P(), P())
    return jax.shard_map(body, mesh=mesh, in_specs=in_specs, out_specs=(split, split), check_vma=False)
```

time: 71.9 us -> 57.1 us (0.79)
  matrix products: 25.6 us -> 8.59 us
  Pallas kernels: 27.1 us -> 33.8 us
  waiting for transfers between devices: 3.73 us -> 0.01 us
  local copies, waits for them, and re-layouts: 5.93 us -> 3.14 us
  other arithmetic: 0.13 us -> 2.69 us
    dot_general x3 -> x1, matrix products: 16.1 us -> 1.63 us  [body(): jnp.dot(jnp.concatenate([embedding, above_embedding], axis=0), short_weig...]
    pallas_call x1, Pallas kernels: 27.1 us -> 33.8 us  [reduced(): pl.pallas_call(functools.partial(reduce_kernel, groups, depth, inv_root),...]
    broadcast_in_dim x2 -> x0, local copies, waits for them, and re-layouts: 4.5 us -> none  [the longest x1 4.46 us: body(): jnp.repeat(jnp.repeat(times, TILE, axis=0), TILE, axis=1)]
    ppermute x3 -> x2, waiting for transfers between devices: 3.73 us -> 0.01 us  [shifted(): lax.ppermute(value, axis, [(i, (i + by) % size) for i in range(size)])]
    dot_general x1, matrix products: 2.6 us -> 1.28 us  [body(): long_range = jnp.dot(table, coeffs, preferred_element_type=jnp.float32)]
    dot_general x1, matrix products: 2.36 us -> 1.12 us  [body(): lax.dot_general(near_grad, short_weight, (((1,), (1,)), ((), ())), prefer...]
    convert_element_type x0 -> x2, other arithmetic: none -> 1 us  [the longest x1 0.97 us: body(): message = (long_range[:, :channels] + forward).astype(jnp.bfloat16)]
    transpose x0 -> x1, local copies, waits for them, and re-layouts: none -> 0.98 us  [body(): left = jnp.concatenate([high, high, low], axis=0)[:, :atom_rows].T]
  transfers between devices with their start and end apart: 3 -> 2, of which waited for: 1 -> 0; matrix products, arithmetic and copies ran while one was open for 40% -> 15% of each run, Pallas kernels for 38% -> 0%
where the time goes in v3:
time: 57.1 us; the launch traced here: 56.9 us
  Pallas kernels  33.8 us (59%)
  matrix products  8.59 us (15%)
  starting transfers between devices  7.1 us (12%)
  local copies, waits for them, and re-layouts  3.14 us (5%)
  other arithmetic  2.69 us (5%)
  between operations  1.52 us (3%)
    pallas_call x1, Pallas kernels, reduced(): pl.pallas_call(functools.partial(reduce_kernel, groups, depth, inv_root),...  33.8 us
    ppermute x2, starting transfers between devices, shifted(): lax.ppermute(value, axis, [(i, (i + by) % size) for i in range(size)])  7.1 us
    dot_general x1, matrix products, trig_table(): lax.dot_general(places, wave_index.astype(jnp.bfloat16), (((0,), (0,)), (...  3.06 us
    dot_general x1, matrix products, body(): jnp.dot(jnp.concatenate([embedding, above_embedding], axis=0), short_weig...  1.63 us
    dot_general x1, matrix products, body(): long_range = jnp.dot(table, coeffs, preferred_element_type=jnp.float32)  1.28 us
    dot_general x1, matrix products, body(): lax.dot_general(table, joined, (((0,), (0,)), ((), ())), preferred_elemen...  1.25 us
  transfers between devices with their start and end apart: 2, of which 0 were waited for; matrix products, arithmetic and copies ran while one was open for 15% of the time, Pallas kernels for 0%

profile of v3, /device:TPU:0, one launch (start us, length us, event | category | flops | bytes accessed | tf_op | source)
XLA Modules:
  0.0 56.9 jit_solution(16154369568318614059)
XLA Ops:
  0.6 0.0 copy-start
  0.6 6.4 %collective-permute-start = (bf16[3,1024]{1,0:T(4,128)(2,1)}, bf16[3,1024]{1,0:T(4,128)(2,1)S(1)}, u32[]{:S(2)}, u32[]{:S(2)}) collective-permute-start(bf16[3,1024]{1,0:T(4,128)(2,1)} %param.10), channel_id=1, source_target_pairs={{0,31},{1,0},{2,1},{3,2},{4,3},{5,4},{6,5},{7,6},{8,7},{9,8},{10,9... | collective-permute-start | bytes 18440 | tf_op jit(solution)/shard_map/ppermute | solution.py:17
  7.1 0.7 %collective-permute-start.1 = (bf16[1024,256]{1,0:T(8,128)(2,1)}, bf16[1024,256]{1,0:T(8,128)(2,1)}, u32[]{:S(2)}, u32[]{:S(2)}) collective-permute-start(bf16[1024,256]{1,0:T(8,128)(2,1)} %param.8), channel_id=1, source_target_pairs={{0,31},{1,0},{2,1},{3,2},{4,3},{5,4},{6,5},{7,6},{8,7},{9,8},{10,9... | collective-permute-start | bytes 1572872 | tf_op jit(solution)/shard_map/ppermute | solution.py:17
  8.4 0.8 %slice_bitcast_fusion.1 = (s32[24]{0:T(128)S(1)}, s32[24]{0:T(128)S(1)}) fusion(s32[24,2]{0,1:T(2,128)} %param.12), kind=kLoop, calls=%fused_computation.64 | loop fusion | bytes 384 | tf_op jit(solution)/shard_map/eq | solution.py:204
  9.2 0.3 fusion.26
  9.4 0.7 %broadcast_bitcast_fusion.times_ref = f32[8,2048]{1,0:T(8,128)} fusion(f32[8,16]{0,1:T(8,128)S(1)} %fusion.26), kind=kLoop, calls=%fused_computation.46 | loop fusion | bytes 66048 | tf_op jit(solution)/shard_map/reshape | solution.py:207
  10.1 0.0 copy-start.1
  10.1 0.0 copy-start.8
  10.1 3.1 %fusion.2 = (bf16[1024,512]{0,1:T(8,128)(2,1)S(1)}, bf16[1024,512]{0,1:T(8,128)(2,1)S(1)}) fusion(bf16[3,1024]{1,0:T(4,128)(2,1)} %param.10, s32[3,512]{1,0:T(4,128)} %param.11), kind=kOutput, calls=%fused_computation.8 | convolution fusion | flops 19400192 | bytes 2109440 | tf_op jit(solution)/shard_map/dot_general | solution.py:32
  13.2 0.0 copy-start.9
  13.2 0.0 copy-start.11
  13.2 0.0 copy-done.1
  13.2 0.0 copy-done.8
  13.3 0.0 copy-start.7
  13.3 1.2 %fusion.36 = (bf16[1024,512]{1,0:T(8,128)(2,1)S(1)}, f32[1024,512]{1,0:T(8,128)S(1)}) fusion(bf16[1024,256]{1,0:T(8,128)(2,1)S(1)} %copy-done.1, bf16[1024,256]{1,0:T(8,128)(2,1)S(1)} %copy-done.8, bf16[1024,512]{0,1:T(8,128)(2,1)S(1)} %get-tuple-element.11, bf16[1024,512]{0,1:T(8,128)(2,1)S(1)} %get-tuple-element.10), kind=kOutput, calls=%fused_computation.68 | convolution fusion | flops 1080557568 | bytes 6291456 | tf_op jit(solution)/shard_map/dot_general | solution.py:191
  14.5 0.0 copy-done.9
  14.5 0.0 copy-done.11
  14.5 0.0 collective-permute-done
  14.5 0.0 copy-done.7
  14.6 0.1 fusion.21
  14.6 0.1 multiply_multiply_fusion.6
  14.7 0.0 copy-start.5
  14.7 0.0 copy-start.6
  14.7 0.6 %copy-done.5 = bf16[6,2048]{1,0:T(8,128)(2,1)} copy-done((bf16[6,2048]{1,0:T(8,128)(2,1)}, bf16[6,2048]{1,0:T(8,128)(2,1)S(1)}, u32[]{:S(2)}) %copy-start.5) | copy-done | bytes 24600
  15.3 0.0 copy-done.6
  15.3 0.6 %fusion.19 = bf16[1024,18]{0,1:T(8,128)(2,1)} fusion(bf16[6,2048]{1,0:T(8,128)(2,1)S(1)} %get-tuple-element.13, bf16[6,2048]{1,0:T(8,128)(2,1)S(1)} %get-tuple-element.12), kind=kLoop, calls=%fused_computation.36 | loop fusion | flops 110592 | bytes 86016 | tf_op jit(solution)/shard_map/transpose | solution.py:201
  16.0 1.0 %copy.11.left_ref = bf16[1024,18]{1,0:T(8,128)(2,1)S(1)} copy(bf16[1024,18]{0,1:T(8,128)(2,1)} %fusion.19) | data formatting | bytes 73728 | tf_op jit(solution)/shard_map/transpose | solution.py:201
  17.0 0.0 copy-start.2
  17.0 0.0 copy-start.3
  17.0 0.0 copy-start.4
  17.0 0.9 %fusion.17.right_ref = bf16[18,2048]{1,0:T(8,128)(2,1)S(1)} fusion(bf16[6,2048]{1,0:T(8,128)(2,1)} %copy-done.5, bf16[6,2048]{1,0:T(8,128)(2,1)} %copy-done.6), kind=kLoop, calls=%fused_computation.30 | loop fusion | flops 221184 | bytes 122880 | tf_op jit(solution)/shard_map/concatenate | solution.py:202
  17.9 0.0 collective-permute-done.1
  17.9 0.0 copy-done
  17.9 1.6 %convolution_convert_fusion.sources_ref = bf16[2048,256]{1,0:T(8,128)(2,1)S(1)} fusion(bf16[256,256]{1,0:T(8,128)(2,1)S(1)} %copy-done, bf16[1024,256]{1,0:T(8,128)(2,1)} %collective-permute-done.1, bf16[1024,256]{1,0:T(8,128)(2,1)} %param.8), kind=kOutput, calls=%fused_computation.5 | convolution fusion | flops 271056896 | bytes 2228224 | tf_op jit(solution)/shard_map/dot_general | solution.py:193
  19.6 0.0 copy-done.2
  19.6 0.0 copy-done.3
  19.6 0.0 copy-done.4
  19.6 0.0 copy-start.10
  19.6 0.0 copy-start.12
  19.6 33.8 %shard_map.95 = (bf16[1024,512]{1,0:T(8,128)(2,1)S(1)}, f32[1024,256]{1,0:T(8,128)S(1)}, bf16[1024,256]{1,0:T(8,128)(2,1)S(1)}) custom-call(f32[1024,512]{1,0:T(8,128)S(1)} %get-tuple-element.17.part_ref, bf16[1024,512]{1,0:T(8,128)(2,1)S(1)} %get-tuple-element.16.sent_ref, f32[512,256]{1,0:T(8,128)S(1)} %copy-done.3, bf16[1024,18]{1,0:T(8,128)(2,1)S(1)} %copy.11.left_ref, ...), custom_call_target="tpu_custom_call" | custom-call | flops 2097152 | bytes 4194304 | tf_op jit(solution)/shard_map/pallas_call | solution.py:154
  53.5 0.0 copy-done.10
  53.5 0.0 copy-done.12
  53.5 1.3 %fusion.7 = f32[1024,512]{1,0:T(8,128)S(1)} fusion(bf16[1024,512]{1,0:T(8,128)(2,1)S(1)} %get-tuple-element.5, bf16[1024,512]{0,1:T(8,128)(2,1)S(1)} %copy-done.12, bf16[1024,512]{0,1:T(8,128)(2,1)S(1)} %copy-done.10), kind=kOutput, calls=%fused_computation.18 | convolution fusion | flops 1077936128 | bytes 5242880 | tf_op jit(solution)/shard_map/dot_general | solution.py:210
  54.8 1.0 %fusion.10 = bf16[1024,256]{1,0:T(8,128)(2,1)} fusion(f32[1024,256]{1,0:T(8,128)S(1)} %get-tuple-element.6, f32[1024,512]{1,0:T(8,128)S(1)} %fusion.7), kind=kLoop, calls=%fused_computation.22 | loop fusion | flops 524288 | bytes 2621440 | tf_op jit(solution)/shard_map/convert_element_type | solution.py:211
  55.8 1.1 %fusion.9 = bf16[1024,256]{1,0:T(8,128)(2,1)} fusion(bf16[1024,256]{1,0:T(8,128)(2,1)S(1)} %get-tuple-element.7, bf16[256,256]{1,0:T(8,128)(2,1)S(1)} %copy-done, f32[1024,512]{1,0:T(8,128)S(1)} %fusion.7), kind=kOutput, calls=%fused_computation.20 | convolution fusion | flops 134742016 | bytes 2228224 | tf_op jit(solution)/shard_map/dot_general | solution.py:209
  (2 shorter events, 0.0 us)
Async XLA Ops:
  0.6 17.3 %copy-start = (bf16[256,256]{1,0:T(8,128)(2,1)S(1)}, bf16[256,256]{1,0:T(8,128)(2,1)}, u32[]{:S(2)}) copy-start(bf16[256,256]{1,0:T(8,128)(2,1)} %param.15) | copy-start | bytes 393220
  0.6 13.9 %collective-permute-start = (bf16[3,1024]{1,0:T(4,128)(2,1)}, bf16[3,1024]{1,0:T(4,128)(2,1)S(1)}, u32[]{:S(2)}, u32[]{:S(2)}) collective-permute-start(bf16[3,1024]{1,0:T(4,128)(2,1)} %param.10), channel_id=1, source_target_pairs={{0,31},{1,0},{2,1},{3,2},{4,3},{5,4},{6,5},{7,6},{8,7},{9,8},{10,9... | collective-permute-start | bytes 18440 | tf_op jit(solution)/shard_map/ppermute | solution.py:17
  7.1 10.9 %collective-permute-start.1 = (bf16[1024,256]{1,0:T(8,128)(2,1)}, bf16[1024,256]{1,0:T(8,128)(2,1)}, u32[]{:S(2)}, u32[]{:S(2)}) collective-permute-start(bf16[1024,256]{1,0:T(8,128)(2,1)} %param.8), channel_id=1, source_target_pairs={{0,31},{1,0},{2,1},{3,2},{4,3},{5,4},{6,5},{7,6},{8,7},{9,8},{10,9... | collective-permute-start | bytes 1572872 | tf_op jit(solution)/shard_map/ppermute | solution.py:17
  10.1 3.1 %copy-start.1 = (bf16[1024,256]{1,0:T(8,128)(2,1)S(1)}, bf16[1024,256]{1,0:T(8,128)(2,1)}, u32[]{:S(2)}) copy-start(bf16[1024,256]{1,0:T(8,128)(2,1)} %cot_ref.1) | copy-start | bytes 1572868
  10.1 3.1 %copy-start.8 = (bf16[1024,256]{1,0:T(8,128)(2,1)S(1)}, bf16[1024,256]{1,0:T(8,128)(2,1)}, u32[]{:S(2)}) copy-start(bf16[1024,256]{1,0:T(8,128)(2,1)} %param.8) | copy-start | bytes 1572868
  13.2 1.3 %copy-start.9 = (bf16[1024,512]{0,1:T(8,128)(2,1)}, bf16[1024,512]{0,1:T(8,128)(2,1)S(1)}, u32[]{:S(2)}) copy-start(bf16[1024,512]{0,1:T(8,128)(2,1)S(1)} %get-tuple-element.10) | copy-start | bytes 3145732
  13.2 1.3 %copy-start.11 = (bf16[1024,512]{0,1:T(8,128)(2,1)}, bf16[1024,512]{0,1:T(8,128)(2,1)S(1)}, u32[]{:S(2)}) copy-start(bf16[1024,512]{0,1:T(8,128)(2,1)S(1)} %get-tuple-element.11) | copy-start | bytes 3145732
  13.3 1.3 %copy-start.7 = (bf16[3,1024]{1,0:T(4,128)(2,1)S(1)}, bf16[3,1024]{1,0:T(4,128)(2,1)}, u32[]{:S(2)}) copy-start(bf16[3,1024]{1,0:T(4,128)(2,1)} %param.10) | copy-start | bytes 18436
  14.7 0.6 %copy-start.5 = (bf16[6,2048]{1,0:T(8,128)(2,1)}, bf16[6,2048]{1,0:T(8,128)(2,1)S(1)}, u32[]{:S(2)}) copy-start(bf16[6,2048]{1,0:T(8,128)(2,1)S(1)} %get-tuple-element.12) | copy-start | bytes 73732
  14.7 0.6 %copy-start.6 = (bf16[6,2048]{1,0:T(8,128)(2,1)}, bf16[6,2048]{1,0:T(8,128)(2,1)S(1)}, u32[]{:S(2)}) copy-start(bf16[6,2048]{1,0:T(8,128)(2,1)S(1)} %get-tuple-element.13) | copy-start | bytes 73732
  17.0 2.6 %copy-start.2 = (bf16[1024,256]{1,0:T(8,128)(2,1)S(1)}, bf16[1024,256]{1,0:T(8,128)(2,1)}, u32[]{:S(2)}) copy-start(bf16[1024,256]{1,0:T(8,128)(2,1)} %cot_ref.1) | copy-start | bytes 1572868
  17.0 2.6 %copy-start.3 = (f32[512,256]{1,0:T(8,128)S(1)}, f32[512,256]{1,0:T(8,128)}, u32[]{:S(2)}) copy-start(f32[512,256]{1,0:T(8,128)} %filter_ref.1) | copy-start | bytes 1572868
  17.0 2.6 %copy-start.4 = (f32[8,2048]{1,0:T(8,128)S(1)}, f32[8,2048]{1,0:T(8,128)}, u32[]{:S(2)}) copy-start(f32[8,2048]{1,0:T(8,128)} %broadcast_bitcast_fusion.times_ref) | copy-start | bytes 196612
  19.6 33.9 %copy-start.10 = (bf16[1024,512]{0,1:T(8,128)(2,1)S(1)}, bf16[1024,512]{0,1:T(8,128)(2,1)}, u32[]{:S(2)}) copy-start(bf16[1024,512]{0,1:T(8,128)(2,1)} %copy-done.9) | copy-start | bytes 3145732
  19.6 33.9 %copy-start.12 = (bf16[1024,512]{0,1:T(8,128)(2,1)S(1)}, bf16[1024,512]{0,1:T(8,128)(2,1)}, u32[]{:S(2)}) copy-start(bf16[1024,512]{0,1:T(8,128)(2,1)} %copy-done.11) | copy-start | bytes 3145732

commit v4 on v3

--- a/solution.py
+++ b/solution.py
@@ -10,11 +10,6 @@
 
 TILE = 128
 two_pi = 2.0 * math.pi
-
-
-def shifted(value, axis, by):
-    size = lax.axis_size(axis)
-    return lax.ppermute(value, axis, [(i, (i + by) % size) for i in range(size)])
 
 
 def cos_sin(turns):
@@ -38,7 +33,7 @@
 
 def reduce_kernel(groups, depth, inv_root, part_ref, sent_ref, filter_ref, left_ref, right_ref, times_ref, sources_ref, cot_ref,
                   out_ref, forward_ref, grad_ref, half_wide, half_in, half_sum, group_wide, group_in, group_sum, depth_in,
-                  backward, back_out, back_in, send_sem, recv_sem):
+                  backward, back_out, back_in, all_sources, all_right, send_sem, recv_sem):
     grp, dev = lax.axis_index("grp"), lax.axis_index("dev")
     place, core = dev // 2, dev % 2
     half = part_ref.shape[0] // 2
@@ -63,13 +58,15 @@
     atom_rows = cot_ref.shape[0]
     tiles = atom_rows // TILE
     backward[...] = jnp.zeros_like(backward)
+    all_sources[:atom_rows, :] = sources_ref[...]
+    all_right[:, :atom_rows] = right_ref[...]
 
     def near_tile(u, carry):
         here = span(u * TILE, TILE)
-        closeness = jnp.dot(left_ref[here, :], right_ref[...], preferred_element_type=jnp.float32)
+        closeness = jnp.dot(left_ref[here, :], all_right[...], preferred_element_type=jnp.float32)
         spread = (jnp.exp(closeness - 3.0) * (1.0 / math.sqrt(TILE))).astype(jnp.bfloat16)
         weights = (spread.astype(jnp.float32) * times_ref[pl.ds(u, 1), :]).astype(jnp.bfloat16)
-        forward_ref[here, :] = jnp.dot(weights, sources_ref[...], preferred_element_type=jnp.float32)
+        forward_ref[here, :] = jnp.dot(weights, all_sources[...], preferred_element_type=jnp.float32)
         backward[...] += lax.dot_general(
             weights, cot_ref[here, :], (((0,), (0,)), ((), ())), preferred_element_type=jnp.float32
         )
@@ -97,14 +94,17 @@
         gain = filter_ref[span(start, total.shape[0]), :]
         return (total * jnp.concatenate([gain, gain], axis=1) * inv_root).astype(jnp.bfloat16)
 
-    exchange([(sent_ref.at[span((1 - core) * half, half)], half_in, other)], 0, tiles // 8)
+    exchange([(sent_ref.at[span((1 - core) * half, half)], half_in, other),
+        (sources_ref, all_sources.at[atom_rows:, :], last_id),
+        (right_ref, all_right.at[:, atom_rows:], last_id),
+    ])
     half_wide[...] = part_ref[span(core * half, half), :] + half_in[...].astype(jnp.float32)
     half_sum[...] = half_wide[...].astype(jnp.bfloat16)
 
     exchange([
         (half_sum.at[span(p * rows, rows)], group_in.at[s], who)
         for s, (p, who) in enumerate(zip(group_peers, group_ids))
-    ], tiles // 8, tiles // 2)
+    ], 0, tiles // 2)
     total = half_wide[span(grp * rows, rows), :]
     for s in range(groups - 1):
         total = total + group_in[s].astype(jnp.float32)
@@ -150,7 +150,7 @@
     half = total_rows // 2
     rows = half // groups
     share = rows // depth if rows % depth == 0 and (rows // depth) % 16 == 0 else rows
-    copies = 3 + 2 * (groups - 1) + 2 * (depth - 1)
+    copies = 5 + 2 * (groups - 1) + 2 * (depth - 1)
     return pl.pallas_call(
         functools.partial(reduce_kernel, groups, depth, inv_root),
         out_shape=(
@@ -168,9 +168,11 @@
             pltpu.VMEM((groups - 1, rows, width), jnp.bfloat16),
             pltpu.VMEM((rows, width), jnp.bfloat16),
             pltpu.VMEM((depth - 1, share, width), jnp.bfloat16),
-            pltpu.VMEM(sources.shape, jnp.float32),
+            pltpu.VMEM((2 * sources.shape[0], sources.shape[1]), jnp.float32),
             pltpu.VMEM(cotangent.shape, jnp.bfloat16),
             pltpu.VMEM(cotangent.shape, jnp.bfloat16),
+            pltpu.VMEM((2 * sources.shape[0], sources.shape[1]), jnp.bfloat16),
+            pltpu.VMEM((right.shape[0], 2 * right.shape[1]), jnp.bfloat16),
             pltpu.SemaphoreType.DMA((copies,)),
             pltpu.SemaphoreType.DMA((copies,)),
         ],
@@ -185,21 +187,21 @@
     pair_rows = tile_pairs.shape[0]
     blocks = lax.axis_size("grp") * lax.axis_size("dev")
     inv_root = 1.0 / math.sqrt(atom_rows * blocks)
-    above_embedding, above_places = shifted((embedding, fractional), ("grp", "dev"), -1)
     table = trig_table(fractional, wave_index)
     joined = jnp.concatenate([embedding, cotangent], axis=1)
     part = lax.dot_general(table, joined, (((0,), (0,)), ((), ())), preferred_element_type=jnp.float32)
 
     sources = jnp.dot(
-        jnp.concatenate([embedding, above_embedding], axis=0), short_weight, preferred_element_type=jnp.float32
+        embedding, short_weight, preferred_element_type=jnp.float32
     ).astype(jnp.bfloat16)
-    cosine, sine = cos_sin(jnp.concatenate([fractional, above_places], axis=1).astype(jnp.float32))
+    cosine, sine = cos_sin(fractional.astype(jnp.float32))
     waves = jnp.concatenate([cosine, sine], axis=0)
     high = lax.reduce_precision(waves, 8, 7)
     low = (waves - high).astype(jnp.bfloat16)
     high = high.astype(jnp.bfloat16)
-    left = jnp.concatenate([high, high, low], axis=0)[:, :atom_rows].T
-    right = jnp.concatenate([high, low, high], axis=0)
+    fill = jnp.zeros((-3 * high.shape[0] % 16, atom_rows), jnp.bfloat16)
+    left = jnp.concatenate([high, high, low, fill], axis=0).T
+    right = jnp.concatenate([high, low, high, fill], axis=0)
     live = (jnp.arange(pair_rows, dtype=jnp.int32) < counts[0])[:, None]
     first_hot = ((tile_pairs[:, :1] == jnp.arange(tiles, dtype=jnp.int32)) & live).astype(jnp.float32)
     second_hot = (tile_pairs[:, 1:] == jnp.arange(2 * tiles, dtype=jnp.int32)).astype(jnp.float32)

time: 57.1 us -> 57.5 us (level)
  Pallas kernels: 33.8 us -> 44.4 us
  starting transfers between devices: 7.1 us -> 0 us
  local copies, waits for them, and re-layouts: 3.14 us -> 1.12 us
  matrix products: 8.59 us -> 7.72 us
    pallas_call x1, Pallas kernels: 33.8 us -> 44.4 us  [reduced(): pl.pallas_call(functools.partial(reduce_kernel, groups, depth, inv_root),...]
    ppermute x2 -> x0, starting transfers between devices: 7.1 us -> none  [shifted(): lax.ppermute(value, axis, [(i, (i + by) % size) for i in range(size)])]
    concatenate x1, other arithmetic: 0.92 us -> 0.09 us  [body(): right = jnp.concatenate([high, low, high, fill], axis=0)]
    transpose x1, local copies, waits for them, and re-layouts: 0.98 us -> 0.17 us  [body(): left = jnp.concatenate([high, high, low, fill], axis=0).T]
    mul x1, other arithmetic: 0.05 us -> 0.73 us  [cos_sin(): sine, cosine = (2.0 * sine * cosine, 1.0 - 2.0 * sine * sine)]
    sub x1, other arithmetic: 0.07 us -> 0.74 us  [cos_sin(): sine, cosine = (2.0 * sine * cosine, 1.0 - 2.0 * sine * sine)]
    reshape x1, local copies, waits for them, and re-layouts: 0.72 us -> 0.08 us  [body(): times = jnp.repeat(times, TILE, axis=1)]
    transpose x1 -> x0, other arithmetic: 0.64 us -> none  [body(): left = jnp.concatenate([high, high, low], axis=0)[:, :atom_rows].T]
  transfers between devices with their start and end apart: 2 -> 0, of which waited for: 0 -> 0; matrix products, arithmetic and copies ran while one was open for 15% -> 0% of each run, Pallas kernels for 0% -> 0%
where the time goes in v4:
time: 57.5 us; the launch traced here: 57.2 us
  Pallas kernels  44.4 us (77%)
  matrix products  7.72 us (13%)
  other arithmetic  2.51 us (4%)
  between operations  1.48 us (3%)
  local copies, waits for them, and re-layouts  1.12 us (2%)
    pallas_call x1, Pallas kernels, reduced(): pl.pallas_call(functools.partial(reduce_kernel, groups, depth, inv_root),...  44.4 us
    dot_general x1, matrix products, trig_table(): lax.dot_general(places, wave_index.astype(jnp.bfloat16), (((0,), (0,)), (...  2.49 us
    dot_general x1, matrix products, body(): jnp.dot(embedding, short_weight, preferred_element_type=jnp.float32)  1.33 us
    dot_general x1, matrix products, body(): long_range = jnp.dot(table, coeffs, preferred_element_type=jnp.float32)  1.28 us
    dot_general x1, matrix products, body(): lax.dot_general(table, joined, (((0,), (0,)), ((), ())), preferred_elemen...  1.25 us

profile of v4, /device:TPU:0, one launch (start us, length us, event | category | flops | bytes accessed | tf_op | source)
XLA Modules:
  0.0 57.2 jit_solution(13256612468387366828)
XLA Ops:
  0.6 0.0 copy-start
  0.6 0.0 copy-start.4
  0.7 0.0 copy-start.5
  1.4 0.1 pad.7.clone
  1.4 0.8 %slice_bitcast_fusion.1 = (s32[24]{0:T(128)S(1)}, s32[24]{0:T(128)S(1)}) fusion(s32[24,2]{0,1:T(2,128)} %param.12), kind=kLoop, calls=%fused_computation.62 | loop fusion | bytes 384 | tf_op jit(solution)/shard_map/eq | solution.py:206
  2.2 0.3 fusion.26
  2.5 0.7 %fusion.21 = (f32[3,1024]{1,0:T(4,128)S(1)}, f32[3,1024]{1,0:T(4,128)S(1)}) fusion(bf16[3,1024]{1,0:T(4,128)(2,1)} %param.10), kind=kLoop, calls=%fused_computation.44 | loop fusion | flops 82944 | bytes 30720 | tf_op jit(solution)/shard_map/sub | solution.py:22
  3.2 0.7 %multiply_multiply_fusion.6 = f32[3,1024]{1,0:T(4,128)S(1)} fusion(f32[3,1024]{1,0:T(4,128)S(1)} %get-tuple-element.9, bf16[3,1024]{1,0:T(4,128)(2,1)} %param.10), kind=kLoop, calls=%fused_computation.39 | loop fusion | flops 58368 | bytes 30720 | tf_op jit(solution)/shard_map/mul | solution.py:22
  3.9 0.1 broadcast_bitcast_fusion.times_ref
  4.0 0.1 fusion.18
  4.1 0.2 copy.11.left_ref
  4.3 0.0 copy-done
  4.3 1.3 %convolution_convert_fusion.sources_ref = bf16[1024,256]{1,0:T(8,128)(2,1)S(1)} fusion(bf16[1024,256]{1,0:T(8,128)(2,1)} %param.8, bf16[256,256]{1,0:T(8,128)(2,1)S(1)} %copy-done), kind=kOutput, calls=%fused_computation.19 | convolution fusion | flops 134479872 | bytes 1179648 | tf_op jit(solution)/shard_map/dot_general | solution.py:194
  5.6 0.0 copy-done.4
  5.7 0.0 copy-done.5
  5.7 0.0 copy-start.1
  5.7 0.0 copy-start.3
  5.7 2.5 %fusion.2 = (bf16[1024,512]{0,1:T(8,128)(2,1)S(1)}, bf16[1024,512]{0,1:T(8,128)(2,1)S(1)}) fusion(bf16[3,1024]{1,0:T(4,128)(2,1)S(1)} %copy-done.4, s32[3,512]{1,0:T(4,128)S(1)} %copy-done.5), kind=kOutput, calls=%fused_computation.7 | convolution fusion | flops 19400192 | bytes 2109440 | tf_op jit(solution)/shard_map/dot_general | solution.py:27
  8.2 0.0 copy-done.1
  8.2 0.0 copy-done.3
  8.2 0.0 copy-start.2
  8.2 1.2 %fusion.35 = (bf16[1024,512]{1,0:T(8,128)(2,1)S(1)}, f32[1024,512]{1,0:T(8,128)S(1)}) fusion(bf16[1024,256]{1,0:T(8,128)(2,1)S(1)} %copy-done.1, bf16[1024,256]{1,0:T(8,128)(2,1)S(1)} %copy-done.3, bf16[1024,512]{0,1:T(8,128)(2,1)S(1)} %get-tuple-element.11, bf16[1024,512]{0,1:T(8,128)(2,1)S(1)} %get-tuple-element.10), kind=kOutput, calls=%fused_computation.65 | convolution fusion | flops 1080557568 | bytes 6291456 | tf_op jit(solution)/shard_map/dot_general | solution.py:192
  9.5 0.0 copy-done.2
  9.5 44.4 %shard_map.95 = (bf16[1024,512]{1,0:T(8,128)(2,1)S(1)}, f32[1024,256]{1,0:T(8,128)S(1)}, bf16[1024,256]{1,0:T(8,128)(2,1)S(1)}) custom-call(f32[1024,512]{1,0:T(8,128)S(1)} %get-tuple-element.19.part_ref, bf16[1024,512]{1,0:T(8,128)(2,1)S(1)} %get-tuple-element.18.sent_ref, f32[512,256]{1,0:T(8,128)S(1)} %copy-done.2, bf16[1024,32]{1,0:T(8,128)(2,1)S(1)} %copy.11.left_ref, ...), custom_call_target="tpu_custom_call" | custom-call | flops 2097152 | bytes 4194304 | tf_op jit(solution)/shard_map/pallas_call | solution.py:154
  53.9 1.3 %fusion.7 = f32[1024,512]{1,0:T(8,128)S(1)} fusion(bf16[1024,512]{1,0:T(8,128)(2,1)S(1)} %get-tuple-element.5, bf16[1024,512]{0,1:T(8,128)(2,1)S(1)} %get-tuple-element.11, bf16[1024,512]{0,1:T(8,128)(2,1)S(1)} %get-tuple-element.10), kind=kOutput, calls=%fused_computation.17 | convolution fusion | flops 1077936128 | bytes 5242880 | tf_op jit(solution)/shard_map/dot_general | solution.py:212
  55.2 0.9 %fusion.10 = bf16[1024,256]{1,0:T(8,128)(2,1)} fusion(f32[1024,256]{1,0:T(8,128)S(1)} %get-tuple-element.6, f32[1024,512]{1,0:T(8,128)S(1)} %fusion.7), kind=kLoop, calls=%fused_computation.22 | loop fusion | flops 524288 | bytes 2621440 | tf_op jit(solution)/shard_map/convert_element_type | solution.py:213
  56.1 1.1 %fusion.9 = bf16[1024,256]{1,0:T(8,128)(2,1)} fusion(bf16[1024,256]{1,0:T(8,128)(2,1)S(1)} %get-tuple-element.7, bf16[256,256]{1,0:T(8,128)(2,1)S(1)} %copy-done, f32[1024,512]{1,0:T(8,128)S(1)} %fusion.7), kind=kOutput, calls=%fused_computation.20 | convolution fusion | flops 134742016 | bytes 2228224 | tf_op jit(solution)/shard_map/dot_general | solution.py:211
  (3 shorter events, 0.0 us)
Async XLA Ops:
  0.6 3.7 %copy-start = (bf16[256,256]{1,0:T(8,128)(2,1)S(1)}, bf16[256,256]{1,0:T(8,128)(2,1)}, u32[]{:S(2)}) copy-start(bf16[256,256]{1,0:T(8,128)(2,1)} %param.15) | copy-start | bytes 393220
  0.6 5.0 %copy-start.4 = (bf16[3,1024]{1,0:T(4,128)(2,1)S(1)}, bf16[3,1024]{1,0:T(4,128)(2,1)}, u32[]{:S(2)}) copy-start(bf16[3,1024]{1,0:T(4,128)(2,1)} %param.10) | copy-start | bytes 18436
  0.7 5.0 %copy-start.5 = (s32[3,512]{1,0:T(4,128)S(1)}, s32[3,512]{1,0:T(4,128)}, u32[]{:S(2)}) copy-start(s32[3,512]{1,0:T(4,128)} %param.11) | copy-start | bytes 18436
  5.7 2.5 %copy-start.1 = (bf16[1024,256]{1,0:T(8,128)(2,1)S(1)}, bf16[1024,256]{1,0:T(8,128)(2,1)}, u32[]{:S(2)}) copy-start(bf16[1024,256]{1,0:T(8,128)(2,1)} %cot_ref.1) | copy-start | bytes 1572868
  5.7 2.5 %copy-start.3 = (bf16[1024,256]{1,0:T(8,128)(2,1)S(1)}, bf16[1024,256]{1,0:T(8,128)(2,1)}, u32[]{:S(2)}) copy-start(bf16[1024,256]{1,0:T(8,128)(2,1)} %param.8) | copy-start | bytes 1572868
  8.2 1.3 %copy-start.2 = (f32[512,256]{1,0:T(8,128)S(1)}, f32[512,256]{1,0:T(8,128)}, u32[]{:S(2)}) copy-start(f32[512,256]{1,0:T(8,128)} %filter_ref.1) | copy-start | bytes 1572868

commit v5 on v4

--- a/solution.py
+++ b/solution.py
@@ -33,7 +33,7 @@
 
 def reduce_kernel(groups, depth, inv_root, part_ref, sent_ref, filter_ref, left_ref, right_ref, times_ref, sources_ref, cot_ref,
                   out_ref, forward_ref, grad_ref, half_wide, half_in, half_sum, group_wide, group_in, group_sum, depth_in,
-                  backward, back_out, back_in, all_sources, all_right, send_sem, recv_sem):
+                  backward, back_out, back_in, sources_in, right_in, send_sem, recv_sem):
     grp, dev = lax.axis_index("grp"), lax.axis_index("dev")
     place, core = dev // 2, dev % 2
     half = part_ref.shape[0] // 2
@@ -58,24 +58,29 @@
     atom_rows = cot_ref.shape[0]
     tiles = atom_rows // TILE
     backward[...] = jnp.zeros_like(backward)
-    all_sources[:atom_rows, :] = sources_ref[...]
-    all_right[:, :atom_rows] = right_ref[...]
-
-    def near_tile(u, carry):
-        here = span(u * TILE, TILE)
-        closeness = jnp.dot(left_ref[here, :], all_right[...], preferred_element_type=jnp.float32)
-        spread = (jnp.exp(closeness - 3.0) * (1.0 / math.sqrt(TILE))).astype(jnp.bfloat16)
-        weights = (spread.astype(jnp.float32) * times_ref[pl.ds(u, 1), :]).astype(jnp.bfloat16)
-        forward_ref[here, :] = jnp.dot(weights, all_sources[...], preferred_element_type=jnp.float32)
-        backward[...] += lax.dot_general(
-            weights, cot_ref[here, :], (((0,), (0,)), ((), ())), preferred_element_type=jnp.float32
-        )
-        return carry
+    forward_ref[...] = jnp.zeros_like(forward_ref)
+
+    def near_tiles(side, first, last):
+        waves, values = ((right_ref, sources_ref), (right_in, sources_in))[side]
+        there = pl.ds(side * atom_rows, atom_rows)
+
+        def near_tile(u, carry):
+            here = span(u * TILE, TILE)
+            closeness = jnp.dot(left_ref[here, :], waves[...], preferred_element_type=jnp.float32)
+            spread = (jnp.exp(closeness - 3.0) * (1.0 / math.sqrt(TILE))).astype(jnp.bfloat16)
+            weights = (spread.astype(jnp.float32) * times_ref[pl.ds(u, 1), there]).astype(jnp.bfloat16)
+            forward_ref[here, :] += jnp.dot(weights, values[...], preferred_element_type=jnp.float32)
+            backward[there, :] += lax.dot_general(
+                weights, cot_ref[here, :], (((0,), (0,)), ((), ())), preferred_element_type=jnp.float32
+            )
+            return carry
+
+        lax.fori_loop(first, last, near_tile, 0)
 
     def span(start, size):
         return pl.ds(pl.multiple_of(start, 16), size)
 
-    def exchange(moves, first=0, last=0):
+    def exchange(moves, side=0, first=0, last=0, wait=True):
         copies = []
         for source, target, who in moves:
             copies.append(pltpu.make_async_remote_copy(
@@ -86,25 +91,27 @@
         for copy in copies:
             copy.start()
         if last > first:
-            lax.fori_loop(first, last, near_tile, 0)
-        for copy in copies:
-            copy.wait()
+            near_tiles(side, first, last)
+        if wait:
+            for copy in copies:
+                copy.wait()
+        return copies
 
     def filtered(total, start):
         gain = filter_ref[span(start, total.shape[0]), :]
         return (total * jnp.concatenate([gain, gain], axis=1) * inv_root).astype(jnp.bfloat16)
 
-    exchange([(sent_ref.at[span((1 - core) * half, half)], half_in, other),
-        (sources_ref, all_sources.at[atom_rows:, :], last_id),
-        (right_ref, all_right.at[:, atom_rows:], last_id),
-    ])
+    neighbour = exchange([(sources_ref, sources_in, last_id), (right_ref, right_in, last_id)], wait=False)
+    exchange([(sent_ref.at[span((1 - core) * half, half)], half_in, other)], 0, 0, tiles // 4)
     half_wide[...] = part_ref[span(core * half, half), :] + half_in[...].astype(jnp.float32)
     half_sum[...] = half_wide[...].astype(jnp.bfloat16)
 
     exchange([
         (half_sum.at[span(p * rows, rows)], group_in.at[s], who)
         for s, (p, who) in enumerate(zip(group_peers, group_ids))
-    ], 0, tiles // 2)
+    ], 0, tiles // 4, tiles * 7 // 8)
+    for copy in neighbour:
+        copy.wait()
     total = half_wide[span(grp * rows, rows), :]
     for s in range(groups - 1):
         total = total + group_in[s].astype(jnp.float32)
@@ -116,15 +123,15 @@
         exchange([
             (group_sum.at[span(p * share, share)], depth_in.at[s], who)
             for s, (p, who) in enumerate(zip(place_peers, place_ids))
-        ], tiles // 2, tiles * 3 // 4)
+        ], 1, 0, tiles // 2)
         total = group_wide[span(place * share, share), :]
         for s in range(depth - 1):
             total = total + depth_in[s].astype(jnp.float32)
         mine = span(base + place * share, share)
         out_ref[mine, :] = filtered(total, grp * rows + place * share)
-        exchange([(out_ref.at[mine], out_ref.at[mine], who) for who in place_ids], tiles * 3 // 4, tiles)
+        exchange([(out_ref.at[mine], out_ref.at[mine], who) for who in place_ids], 1, tiles // 2, tiles)
     else:
-        exchange([(group_sum, depth_in.at[s], who) for s, who in enumerate(place_ids)], tiles // 2, tiles)
+        exchange([(group_sum, depth_in.at[s], who) for s, who in enumerate(place_ids)], 1, 0, tiles)
         total = group_wide[...]
         for s in range(depth - 1):
             total = total + depth_in[s].astype(jnp.float32)
@@ -137,7 +144,7 @@
     used[0] += 1
     back.start()
     mine = span(base, rows)
-    exchange([(out_ref.at[mine], out_ref.at[mine], who) for who in group_ids])
+    exchange([(out_ref.at[mine], out_ref.at[mine], who) for who in group_ids], 0, tiles * 7 // 8, tiles)
     mine = span(core * half, half)
     exchange([(out_ref.at[mine], out_ref.at[mine], other)])
     back.wait()
@@ -171,8 +178,8 @@
             pltpu.VMEM((2 * sources.shape[0], sources.shape[1]), jnp.float32),
             pltpu.VMEM(cotangent.shape, jnp.bfloat16),
             pltpu.VMEM(cotangent.shape, jnp.bfloat16),
-            pltpu.VMEM((2 * sources.shape[0], sources.shape[1]), jnp.bfloat16),
-            pltpu.VMEM((right.shape[0], 2 * right.shape[1]), jnp.bfloat16),
+            pltpu.VMEM(sources.shape, jnp.bfloat16),
+            pltpu.VMEM(right.shape, jnp.bfloat16),
             pltpu.SemaphoreType.DMA((copies,)),
             pltpu.SemaphoreType.DMA((copies,)),
         ],

time: 57.5 us -> 56.4 us (0.981)
  Pallas kernels: 44.4 us -> 43.3 us
    pallas_call x1, Pallas kernels: 44.4 us -> 43.3 us  [reduced(): pl.pallas_call(functools.partial(reduce_kernel, groups, depth, inv_root),...]
where the time goes in v5:
time: 56.4 us; the launch traced here: 56.1 us
  Pallas kernels  43.3 us (77%)
  matrix products  7.73 us (14%)
  other arithmetic  2.51 us (4%)
  between operations  1.48 us (3%)
  local copies, waits for them, and re-layouts  1.12 us (2%)
    pallas_call x1, Pallas kernels, reduced(): pl.pallas_call(functools.partial(reduce_kernel, groups, depth, inv_root),...  43.3 us
    dot_general x1, matrix products, trig_table(): lax.dot_general(places, wave_index.astype(jnp.bfloat16), (((0,), (0,)), (...  2.49 us
    dot_general x1, matrix products, body(): jnp.dot(embedding, short_weight, preferred_element_type=jnp.float32)  1.33 us
    dot_general x1, matrix products, body(): long_range = jnp.dot(table, coeffs, preferred_element_type=jnp.float32)  1.28 us
    dot_general x1, matrix products, body(): lax.dot_general(table, joined, (((0,), (0,)), ((), ())), preferred_elemen...  1.25 us

profile of v5, /device:TPU:0, one launch (start us, length us, event | category | flops | bytes accessed | tf_op | source)
XLA Modules:
  0.0 56.1 jit_solution(5719313374459075981)
XLA Ops:
  0.6 0.0 copy-start
  0.6 0.0 copy-start.4
  0.7 0.0 copy-start.5
  1.4 0.1 pad.7.clone
  1.4 0.8 %slice_bitcast_fusion.1 = (s32[24]{0:T(128)S(1)}, s32[24]{0:T(128)S(1)}) fusion(s32[24,2]{0,1:T(2,128)} %param.12), kind=kLoop, calls=%fused_computation.62 | loop fusion | bytes 384 | tf_op jit(solution)/shard_map/eq | solution.py:213
  2.2 0.3 fusion.26
  2.5 0.7 %fusion.21 = (f32[3,1024]{1,0:T(4,128)S(1)}, f32[3,1024]{1,0:T(4,128)S(1)}) fusion(bf16[3,1024]{1,0:T(4,128)(2,1)} %param.10), kind=kLoop, calls=%fused_computation.44 | loop fusion | flops 82944 | bytes 30720 | tf_op jit(solution)/shard_map/sub | solution.py:22
  3.2 0.7 %multiply_multiply_fusion.6 = f32[3,1024]{1,0:T(4,128)S(1)} fusion(f32[3,1024]{1,0:T(4,128)S(1)} %get-tuple-element.9, bf16[3,1024]{1,0:T(4,128)(2,1)} %param.10), kind=kLoop, calls=%fused_computation.39 | loop fusion | flops 58368 | bytes 30720 | tf_op jit(solution)/shard_map/mul | solution.py:22
  3.9 0.1 broadcast_bitcast_fusion.times_ref
  4.0 0.1 fusion.18
  4.1 0.2 copy.11.left_ref
  4.3 0.0 copy-done
  4.3 1.3 %convolution_convert_fusion.sources_ref = bf16[1024,256]{1,0:T(8,128)(2,1)S(1)} fusion(bf16[1024,256]{1,0:T(8,128)(2,1)} %param.8, bf16[256,256]{1,0:T(8,128)(2,1)S(1)} %copy-done), kind=kOutput, calls=%fused_computation.19 | convolution fusion | flops 134479872 | bytes 1179648 | tf_op jit(solution)/shard_map/dot_general | solution.py:201
  5.6 0.0 copy-done.4
  5.7 0.0 copy-done.5
  5.7 0.0 copy-start.1
  5.7 0.0 copy-start.3
  5.7 2.5 %fusion.2 = (bf16[1024,512]{0,1:T(8,128)(2,1)S(1)}, bf16[1024,512]{0,1:T(8,128)(2,1)S(1)}) fusion(bf16[3,1024]{1,0:T(4,128)(2,1)S(1)} %copy-done.4, s32[3,512]{1,0:T(4,128)S(1)} %copy-done.5), kind=kOutput, calls=%fused_computation.7 | convolution fusion | flops 19400192 | bytes 2109440 | tf_op jit(solution)/shard_map/dot_general | solution.py:27
  8.2 0.0 copy-done.1
  8.2 0.0 copy-done.3
  8.2 0.0 copy-start.2
  8.2 1.2 %fusion.35 = (bf16[1024,512]{1,0:T(8,128)(2,1)S(1)}, f32[1024,512]{1,0:T(8,128)S(1)}) fusion(bf16[1024,256]{1,0:T(8,128)(2,1)S(1)} %copy-done.1, bf16[1024,256]{1,0:T(8,128)(2,1)S(1)} %copy-done.3, bf16[1024,512]{0,1:T(8,128)(2,1)S(1)} %get-tuple-element.11, bf16[1024,512]{0,1:T(8,128)(2,1)S(1)} %get-tuple-element.10), kind=kOutput, calls=%fused_computation.65 | convolution fusion | flops 1080557568 | bytes 6291456 | tf_op jit(solution)/shard_map/dot_general | solution.py:199
  9.5 0.0 copy-done.2
  9.5 43.3 %shard_map.95 = (bf16[1024,512]{1,0:T(8,128)(2,1)S(1)}, f32[1024,256]{1,0:T(8,128)S(1)}, bf16[1024,256]{1,0:T(8,128)(2,1)S(1)}) custom-call(f32[1024,512]{1,0:T(8,128)S(1)} %get-tuple-element.19.part_ref, bf16[1024,512]{1,0:T(8,128)(2,1)S(1)} %get-tuple-element.18.sent_ref, f32[512,256]{1,0:T(8,128)S(1)} %copy-done.2, bf16[1024,32]{1,0:T(8,128)(2,1)S(1)} %copy.11.left_ref, ...), custom_call_target="tpu_custom_call" | custom-call | flops 2097152 | bytes 4194304 | tf_op jit(solution)/shard_map/pallas_call | solution.py:161
  52.8 1.3 %fusion.7 = f32[1024,512]{1,0:T(8,128)S(1)} fusion(bf16[1024,512]{1,0:T(8,128)(2,1)S(1)} %get-tuple-element.5, bf16[1024,512]{0,1:T(8,128)(2,1)S(1)} %get-tuple-element.11, bf16[1024,512]{0,1:T(8,128)(2,1)S(1)} %get-tuple-element.10), kind=kOutput, calls=%fused_computation.17 | convolution fusion | flops 1077936128 | bytes 5242880 | tf_op jit(solution)/shard_map/dot_general | solution.py:219
  54.0 0.9 %fusion.10 = bf16[1024,256]{1,0:T(8,128)(2,1)} fusion(f32[1024,256]{1,0:T(8,128)S(1)} %get-tuple-element.6, f32[1024,512]{1,0:T(8,128)S(1)} %fusion.7), kind=kLoop, calls=%fused_computation.22 | loop fusion | flops 524288 | bytes 2621440 | tf_op jit(solution)/shard_map/convert_element_type | solution.py:220
  55.0 1.1 %fusion.9 = bf16[1024,256]{1,0:T(8,128)(2,1)} fusion(bf16[1024,256]{1,0:T(8,128)(2,1)S(1)} %get-tuple-element.7, bf16[256,256]{1,0:T(8,128)(2,1)S(1)} %copy-done, f32[1024,512]{1,0:T(8,128)S(1)} %fusion.7), kind=kOutput, calls=%fused_computation.20 | convolution fusion | flops 134742016 | bytes 2228224 | tf_op jit(solution)/shard_map/dot_general | solution.py:218
  (3 shorter events, 0.0 us)
Async XLA Ops:
  0.6 3.7 %copy-start = (bf16[256,256]{1,0:T(8,128)(2,1)S(1)}, bf16[256,256]{1,0:T(8,128)(2,1)}, u32[]{:S(2)}) copy-start(bf16[256,256]{1,0:T(8,128)(2,1)} %param.15) | copy-start | bytes 393220
  0.6 5.0 %copy-start.4 = (bf16[3,1024]{1,0:T(4,128)(2,1)S(1)}, bf16[3,1024]{1,0:T(4,128)(2,1)}, u32[]{:S(2)}) copy-start(bf16[3,1024]{1,0:T(4,128)(2,1)} %param.10) | copy-start | bytes 18436
  0.7 5.0 %copy-start.5 = (s32[3,512]{1,0:T(4,128)S(1)}, s32[3,512]{1,0:T(4,128)}, u32[]{:S(2)}) copy-start(s32[3,512]{1,0:T(4,128)} %param.11) | copy-start | bytes 18436
  5.7 2.5 %copy-start.1 = (bf16[1024,256]{1,0:T(8,128)(2,1)S(1)}, bf16[1024,256]{1,0:T(8,128)(2,1)}, u32[]{:S(2)}) copy-start(bf16[1024,256]{1,0:T(8,128)(2,1)} %cot_ref.1) | copy-start | bytes 1572868
  5.7 2.5 %copy-start.3 = (bf16[1024,256]{1,0:T(8,128)(2,1)S(1)}, bf16[1024,256]{1,0:T(8,128)(2,1)}, u32[]{:S(2)}) copy-start(bf16[1024,256]{1,0:T(8,128)(2,1)} %param.8) | copy-start | bytes 1572868
  8.2 1.3 %copy-start.2 = (f32[512,256]{1,0:T(8,128)S(1)}, f32[512,256]{1,0:T(8,128)}, u32[]{:S(2)}) copy-start(f32[512,256]{1,0:T(8,128)} %filter_ref.1) | copy-start | bytes 1572868

commit v6 on v5

--- a/solution.py
+++ b/solution.py
@@ -106,11 +106,14 @@
     half_wide[...] = part_ref[span(core * half, half), :] + half_in[...].astype(jnp.float32)
     half_sum[...] = half_wide[...].astype(jnp.bfloat16)
 
-    exchange([
+    pieces = exchange([
         (half_sum.at[span(p * rows, rows)], group_in.at[s], who)
         for s, (p, who) in enumerate(zip(group_peers, group_ids))
-    ], 0, tiles // 4, tiles * 7 // 8)
+    ], 0, tiles // 4, tiles * 5 // 8, wait=False)
     for copy in neighbour:
+        copy.wait()
+    near_tiles(1, 0, tiles // 4)
+    for copy in pieces:
         copy.wait()
     total = half_wide[span(grp * rows, rows), :]
     for s in range(groups - 1):
@@ -123,15 +126,15 @@
         exchange([
             (group_sum.at[span(p * share, share)], depth_in.at[s], who)
             for s, (p, who) in enumerate(zip(place_peers, place_ids))
-        ], 1, 0, tiles // 2)
+        ], 1, tiles // 4, tiles * 5 // 8)
         total = group_wide[span(place * share, share), :]
         for s in range(depth - 1):
             total = total + depth_in[s].astype(jnp.float32)
         mine = span(base + place * share, share)
         out_ref[mine, :] = filtered(total, grp * rows + place * share)
-        exchange([(out_ref.at[mine], out_ref.at[mine], who) for who in place_ids], 1, tiles // 2, tiles)
+        exchange([(out_ref.at[mine], out_ref.at[mine], who) for who in place_ids], 1, tiles * 5 // 8, tiles)
     else:
-        exchange([(group_sum, depth_in.at[s], who) for s, who in enumerate(place_ids)], 1, 0, tiles)
+        exchange([(group_sum, depth_in.at[s], who) for s, who in enumerate(place_ids)], 1, tiles // 4, tiles)
         total = group_wide[...]
         for s in range(depth - 1):
             total = total + depth_in[s].astype(jnp.float32)
@@ -144,9 +147,14 @@
     used[0] += 1
     back.start()
     mine = span(base, rows)
-    exchange([(out_ref.at[mine], out_ref.at[mine], who) for who in group_ids], 0, tiles * 7 // 8, tiles)
-    mine = span(core * half, half)
-    exchange([(out_ref.at[mine], out_ref.at[mine], other)])
+    pieces = exchange([(out_ref.at[mine], out_ref.at[mine], who) for who in group_ids], wait=False)
+    passed = exchange([(out_ref.at[mine], out_ref.at[mine], other)], 0, tiles * 5 // 8, tiles, wait=False)
+    for s, copy in enumerate(pieces):
+        copy.wait()
+        here = span(core * half + lax.rem(grp + groups - 1 - s, groups) * rows, rows)
+        passed += exchange([(out_ref.at[here], out_ref.at[here], other)], wait=False)
+    for copy in passed:
+        copy.wait()
     back.wait()
     grad_ref[...] = (backward[:atom_rows, :] + back_in[...].astype(jnp.float32)).astype(jnp.bfloat16)
 
@@ -157,7 +165,7 @@
     half = total_rows // 2
     rows = half // groups
     share = rows // depth if rows % depth == 0 and (rows // depth) % 16 == 0 else rows
-    copies = 5 + 2 * (groups - 1) + 2 * (depth - 1)
+    copies = 5 + 3 * (groups - 1) + 2 * (depth - 1)
     return pl.pallas_call(
         functools.partial(reduce_kernel, groups, depth, inv_root),
         out_shape=(

time: 56.4 us -> 55.3 us (0.980)
  Pallas kernels: 43.3 us -> 42.1 us
    pallas_call x1, Pallas kernels: 43.3 us -> 42.1 us  [reduced(): pl.pallas_call(functools.partial(reduce_kernel, groups, depth, inv_root),...]
where the time goes in v6:
time: 55.3 us; the launch traced here: 55 us
  Pallas kernels  42.1 us (76%)
  matrix products  7.73 us (14%)
  other arithmetic  2.51 us (5%)
  between operations  1.48 us (3%)
  local copies, waits for them, and re-layouts  1.12 us (2%)
    pallas_call x1, Pallas kernels, reduced(): pl.pallas_call(functools.partial(reduce_kernel, groups, depth, inv_root),...  42.1 us
    dot_general x1, matrix products, trig_table(): lax.dot_general(places, wave_index.astype(jnp.bfloat16), (((0,), (0,)), (...  2.49 us
    dot_general x1, matrix products, body(): jnp.dot(embedding, short_weight, preferred_element_type=jnp.float32)  1.33 us
    dot_general x1, matrix products, body(): long_range = jnp.dot(table, coeffs, preferred_element_type=jnp.float32)  1.28 us
    dot_general x1, matrix products, body(): lax.dot_general(table, joined, (((0,), (0,)), ((), ())), preferred_elemen...  1.25 us
    dot_general x1, matrix products, body(): lax.dot_general(near_grad, short_weight, (((1,), (1,)), ((), ())), prefer...  1.13 us

profile of v6, /device:TPU:0, one launch (start us, length us, event | category | flops | bytes accessed | tf_op | source)
XLA Modules:
  0.0 55.0 jit_solution(8765281369535303616)
XLA Ops:
  0.6 0.0 copy-start
  0.6 0.0 copy-start.4
  0.7 0.0 copy-start.5
  1.4 0.1 pad.7.clone
  1.4 0.8 %slice_bitcast_fusion.1 = (s32[24]{0:T(128)S(1)}, s32[24]{0:T(128)S(1)}) fusion(s32[24,2]{0,1:T(2,128)} %param.12), kind=kLoop, calls=%fused_computation.62 | loop fusion | bytes 384 | tf_op jit(solution)/shard_map/eq | solution.py:221
  2.2 0.3 fusion.26
  2.5 0.7 %fusion.21 = (f32[3,1024]{1,0:T(4,128)S(1)}, f32[3,1024]{1,0:T(4,128)S(1)}) fusion(bf16[3,1024]{1,0:T(4,128)(2,1)} %param.10), kind=kLoop, calls=%fused_computation.44 | loop fusion | flops 82944 | bytes 30720 | tf_op jit(solution)/shard_map/sub | solution.py:22
  3.2 0.7 %multiply_multiply_fusion.6 = f32[3,1024]{1,0:T(4,128)S(1)} fusion(f32[3,1024]{1,0:T(4,128)S(1)} %get-tuple-element.9, bf16[3,1024]{1,0:T(4,128)(2,1)} %param.10), kind=kLoop, calls=%fused_computation.39 | loop fusion | flops 58368 | bytes 30720 | tf_op jit(solution)/shard_map/mul | solution.py:22
  3.9 0.1 broadcast_bitcast_fusion.times_ref
  4.0 0.1 fusion.18
  4.1 0.2 copy.11.left_ref
  4.3 0.0 copy-done
  4.3 1.3 %convolution_convert_fusion.sources_ref = bf16[1024,256]{1,0:T(8,128)(2,1)S(1)} fusion(bf16[1024,256]{1,0:T(8,128)(2,1)} %param.8, bf16[256,256]{1,0:T(8,128)(2,1)S(1)} %copy-done), kind=kOutput, calls=%fused_computation.19 | convolution fusion | flops 134479872 | bytes 1179648 | tf_op jit(solution)/shard_map/dot_general | solution.py:209
  5.6 0.0 copy-done.4
  5.7 0.0 copy-done.5
  5.7 0.0 copy-start.1
  5.7 0.0 copy-start.3
  5.7 2.5 %fusion.2 = (bf16[1024,512]{0,1:T(8,128)(2,1)S(1)}, bf16[1024,512]{0,1:T(8,128)(2,1)S(1)}) fusion(bf16[3,1024]{1,0:T(4,128)(2,1)S(1)} %copy-done.4, s32[3,512]{1,0:T(4,128)S(1)} %copy-done.5), kind=kOutput, calls=%fused_computation.7 | convolution fusion | flops 19400192 | bytes 2109440 | tf_op jit(solution)/shard_map/dot_general | solution.py:27
  8.2 0.0 copy-done.1
  8.2 0.0 copy-done.3
  8.2 0.0 copy-start.2
  8.2 1.2 %fusion.35 = (bf16[1024,512]{1,0:T(8,128)(2,1)S(1)}, f32[1024,512]{1,0:T(8,128)S(1)}) fusion(bf16[1024,256]{1,0:T(8,128)(2,1)S(1)} %copy-done.1, bf16[1024,256]{1,0:T(8,128)(2,1)S(1)} %copy-done.3, bf16[1024,512]{0,1:T(8,128)(2,1)S(1)} %get-tuple-element.11, bf16[1024,512]{0,1:T(8,128)(2,1)S(1)} %get-tuple-element.10), kind=kOutput, calls=%fused_computation.65 | convolution fusion | flops 1080557568 | bytes 6291456 | tf_op jit(solution)/shard_map/dot_general | solution.py:207
  9.5 0.0 copy-done.2
  9.5 42.1 %shard_map.95 = (bf16[1024,512]{1,0:T(8,128)(2,1)S(1)}, f32[1024,256]{1,0:T(8,128)S(1)}, bf16[1024,256]{1,0:T(8,128)(2,1)S(1)}) custom-call(f32[1024,512]{1,0:T(8,128)S(1)} %get-tuple-element.19.part_ref, bf16[1024,512]{1,0:T(8,128)(2,1)S(1)} %get-tuple-element.18.sent_ref, f32[512,256]{1,0:T(8,128)S(1)} %copy-done.2, bf16[1024,32]{1,0:T(8,128)(2,1)S(1)} %copy.11.left_ref, ...), custom_call_target="tpu_custom_call" | custom-call | flops 2097152 | bytes 4194304 | tf_op jit(solution)/shard_map/pallas_call | solution.py:169
  51.6 1.3 %fusion.7 = f32[1024,512]{1,0:T(8,128)S(1)} fusion(bf16[1024,512]{1,0:T(8,128)(2,1)S(1)} %get-tuple-element.5, bf16[1024,512]{0,1:T(8,128)(2,1)S(1)} %get-tuple-element.11, bf16[1024,512]{0,1:T(8,128)(2,1)S(1)} %get-tuple-element.10), kind=kOutput, calls=%fused_computation.17 | convolution fusion | flops 1077936128 | bytes 5242880 | tf_op jit(solution)/shard_map/dot_general | solution.py:227
  52.9 0.9 %fusion.10 = bf16[1024,256]{1,0:T(8,128)(2,1)} fusion(f32[1024,256]{1,0:T(8,128)S(1)} %get-tuple-element.6, f32[1024,512]{1,0:T(8,128)S(1)} %fusion.7), kind=kLoop, calls=%fused_computation.22 | loop fusion | flops 524288 | bytes 2621440 | tf_op jit(solution)/shard_map/convert_element_type | solution.py:228
  53.9 1.1 %fusion.9 = bf16[1024,256]{1,0:T(8,128)(2,1)} fusion(bf16[1024,256]{1,0:T(8,128)(2,1)S(1)} %get-tuple-element.7, bf16[256,256]{1,0:T(8,128)(2,1)S(1)} %copy-done, f32[1024,512]{1,0:T(8,128)S(1)} %fusion.7), kind=kOutput, calls=%fused_computation.20 | convolution fusion | flops 134742016 | bytes 2228224 | tf_op jit(solution)/shard_map/dot_general | solution.py:226
  (3 shorter events, 0.0 us)
Async XLA Ops:
  0.6 3.7 %copy-start = (bf16[256,256]{1,0:T(8,128)(2,1)S(1)}, bf16[256,256]{1,0:T(8,128)(2,1)}, u32[]{:S(2)}) copy-start(bf16[256,256]{1,0:T(8,128)(2,1)} %param.15) | copy-start | bytes 393220
  0.6 5.0 %copy-start.4 = (bf16[3,1024]{1,0:T(4,128)(2,1)S(1)}, bf16[3,1024]{1,0:T(4,128)(2,1)}, u32[]{:S(2)}) copy-start(bf16[3,1024]{1,0:T(4,128)(2,1)} %param.10) | copy-start | bytes 18436
  0.7 5.0 %copy-start.5 = (s32[3,512]{1,0:T(4,128)S(1)}, s32[3,512]{1,0:T(4,128)}, u32[]{:S(2)}) copy-start(s32[3,512]{1,0:T(4,128)} %param.11) | copy-start | bytes 18436
  5.7 2.5 %copy-start.1 = (bf16[1024,256]{1,0:T(8,128)(2,1)S(1)}, bf16[1024,256]{1,0:T(8,128)(2,1)}, u32[]{:S(2)}) copy-start(bf16[1024,256]{1,0:T(8,128)(2,1)} %cot_ref.1) | copy-start | bytes 1572868
  5.7 2.5 %copy-start.3 = (bf16[1024,256]{1,0:T(8,128)(2,1)S(1)}, bf16[1024,256]{1,0:T(8,128)(2,1)}, u32[]{:S(2)}) copy-start(bf16[1024,256]{1,0:T(8,128)(2,1)} %param.8) | copy-start | bytes 1572868
  8.2 1.3 %copy-start.2 = (f32[512,256]{1,0:T(8,128)S(1)}, f32[512,256]{1,0:T(8,128)}, u32[]{:S(2)}) copy-start(f32[512,256]{1,0:T(8,128)} %filter_ref.1) | copy-start | bytes 1572868
